TPU v7x, 512 devices: a whole 4x8x8 slice. The times are simulated.
512 devices in a mesh: grid: 16 (over z_hi, x, core), comp: 32 (over y, z_lo).
Axes of the slice: x: 4, y: 8, z: 8 (z_hi: 2, z_lo: 4; z = z_hi * 4 + z_lo), core: 2. Of those that a mesh axis runs over, the one named last changes fastest.
Arguments:
- spectra: float32 [32, 32, 36, 8192], P('comp', None, None, 'grid'), may hold values from 0.1 to 2
- u_wind: float32 [32, 8192], P(None, 'grid'), may hold values from 2 to 20
- wind_dir: float32 [32, 8192], P(None, 'grid'), may hold values from -3.140625 to 3.140625
- sea_mask: int32 [32, 8192], P(None, 'grid'), may hold values from 0 to 1, as said below
Outputs:
- spectra_next: float32 [32, 32, 36, 8192], P('comp', None, None, 'grid')
Inputs may be any that keep to these rules, and one draw needn't show every extreme that they name: sea_mask is 1 at sea and 0 on land; land lies in rectangular blocks of rows and columns.
All inputs are finite; a program needn't handle non-finite values.
Results may differ from a plain program's by a relative error of at most 0.00016.
Values sent between devices are 32-bit elements; how exact they have to be, the bound alone decides.
A program may use at most 64 MiB of HBM per device.

v0:
```python
import math

import jax
import jax.numpy as jnp
from jax import lax
from jax.sharding import PartitionSpec as P

GRAVITY = 9.81
FREQ_LOW = 0.04
FREQ_RATIO = 1.1
LAMBDA = 0.25
SOURCE_STEP = 120.0
ADVECT_STEP = 220.0
WIND_FACTOR = 0.0003125
TRANSFER_FACTOR = 0.1
EARTH_RADIUS = 6371000.0
BAND_CENTRE = 30.0
CELL_DEGREES = 0.05
CELL_RADIANS = CELL_DEGREES * math.pi / 180.0
ANGLE_NEAR = 11.48
ANGLE_FAR = 33.56
FREQ_UPPER_SHIFT = math.log(1.0 + LAMBDA) / math.log(FREQ_RATIO)
FREQ_LOWER_SHIFT = math.log(1.0 - LAMBDA) / math.log(FREQ_RATIO)
WEIGHT_UPPER = 1.0 / (1.0 + LAMBDA) ** 4
WEIGHT_LOWER = 1.0 / (1.0 - LAMBDA) ** 4
WEIGHT_CROSS = 2.0 / (1.0 - LAMBDA * LAMBDA) ** 4
HIGHEST = lax.Precision.HIGHEST


def padded_2(block, sides, width):
    for axis, dim in sides:
        count = lax.axis_size(axis)
        forward = [(i, i + 1) for i in range(count - 1)]
        backward = [(target, source) for source, target in forward]
        low = lax.ppermute(
            lax.slice_in_dim(block, block.shape[dim] - width, None, axis=dim), axis, forward
        )
        high = lax.ppermute(lax.slice_in_dim(block, 0, width, axis=dim), axis, backward)
        block = jnp.concatenate([low, block, high], axis=dim)
    return block


def hat_matrix(bin_count, bin_shift, periodic):
    target = jnp.arange(bin_count, dtype=jnp.float32)[:, None] + bin_shift
    source = jnp.arange(bin_count, dtype=jnp.float32)[None, :]
    offset_gap = target - source
    if periodic:
        offset_gap = jnp.mod(offset_gap + bin_count / 2.0, float(bin_count)) - bin_count / 2.0
    return jnp.maximum(0.0, 1.0 - jnp.abs(offset_gap))


def nonlinear(point_block):
    freq_count = point_block.shape[0]
    dir_count = point_block.shape[2]
    freq_upper = hat_matrix(freq_count, FREQ_UPPER_SHIFT, False)
    freq_lower = hat_matrix(freq_count, FREQ_LOWER_SHIFT, False)
    spread_upper = jnp.einsum("km,mrjq->krjq", freq_upper, point_block, precision=HIGHEST)
    spread_lower = jnp.einsum("km,mrjq->krjq", freq_lower, point_block, precision=HIGHEST)
    near_bins = ANGLE_NEAR * dir_count / 360.0
    far_bins = ANGLE_FAR * dir_count / 360.0
    squared = point_block * point_block
    centre_total = jnp.zeros_like(point_block)
    back_upper = jnp.zeros_like(point_block)
    back_lower = jnp.zeros_like(point_block)
    for shifts in ((near_bins, -far_bins), (-near_bins, far_bins)):
        dir_upper = hat_matrix(dir_count, shifts[0], True)
        dir_lower = hat_matrix(dir_count, shifts[1], True)
        plus_value = jnp.einsum("jn,krnq->krjq", dir_upper, spread_upper, precision=HIGHEST)
        minus_value = jnp.einsum("jn,krnq->krjq", dir_lower, spread_lower, precision=HIGHEST)
        interaction = TRANSFER_FACTOR * (
            squared * (plus_value * WEIGHT_UPPER + minus_value * WEIGHT_LOWER)
            - WEIGHT_CROSS * point_block * plus_value * minus_value
        )
        centre_total = centre_total - 2.0 * interaction
        back_upper = back_upper + jnp.einsum(
            "jn,krjq->krnq", dir_upper, interaction, precision=HIGHEST
        )
        back_lower = back_lower + jnp.einsum(
            "jn,krjq->krnq", dir_lower, interaction, precision=HIGHEST
        )
    centre_total = centre_total + jnp.einsum(
        "km,krjq->mrjq", freq_upper, back_upper, precision=HIGHEST
    )
    return centre_total + jnp.einsum("km,krjq->mrjq", freq_lower, back_lower, precision=HIGHEST)


def frequency(freq_index):
    return (FREQ_LOW * jnp.power(FREQ_RATIO, freq_index.astype(jnp.float32))).reshape(-1, 1, 1, 1)


def wind_growth(freq, angles, wind_speed, heading):
    radian_freq = 2.0 * math.pi * freq
    celerity = GRAVITY / radian_freq
    alignment = jnp.cos(angles) * jnp.cos(heading) + jnp.sin(angles) * jnp.sin(heading)
    return (
        WIND_FACTOR
        * SOURCE_STEP
        * radian_freq
        * jnp.maximum(0.0, wind_speed / celerity * alignment - 1.0)
    )


def courant_x(freq, angles, row_index, total_rows):
    group_speed = GRAVITY / (4.0 * math.pi * freq)
    latitude = BAND_CENTRE + (row_index.astype(jnp.float32) - (total_rows - 1) / 2.0) * CELL_DEGREES
    row_cos = jnp.cos(latitude * (math.pi / 180.0)).reshape(1, -1, 1, 1)
    return group_speed * jnp.cos(angles) * ADVECT_STEP / (EARTH_RADIUS * row_cos * CELL_RADIANS)


def courant_y(freq, angles):
    group_speed = GRAVITY / (4.0 * math.pi * freq)
    return group_speed * jnp.sin(angles) * ADVECT_STEP / (EARTH_RADIUS * CELL_RADIANS)


def latitude_cos(total_rows):
    cell_lat = (
        BAND_CENTRE
        + (jnp.arange(total_rows, dtype=jnp.float32) - (total_rows - 1) / 2.0) * CELL_DEGREES
    )
    face_lat = (
        BAND_CENTRE
        + (jnp.arange(total_rows + 1, dtype=jnp.float32) - total_rows / 2.0) * CELL_DEGREES
    )
    cell_cos = jnp.cos(cell_lat * (math.pi / 180.0)).reshape(1, -1, 1, 1)
    face_cos = jnp.cos(face_lat * (math.pi / 180.0)).reshape(1, -1, 1, 1)
    return (face_cos, 1.0 / cell_cos)


def advect(padded, courant, face_weight, cell_weight, along_axis):
    cells = padded.shape[along_axis] - 4

    def piece_at(offset_cells, length_cells):
        return lax.slice_in_dim(padded, offset_cells, offset_cells + length_cells, axis=along_axis)

    left_cell = piece_at(1, cells + 1)
    right_cell = piece_at(2, cells + 1)
    far_left = piece_at(0, cells + 1)
    far_right = piece_at(3, cells + 1)
    curvature = jnp.where(
        courant >= 0.0,
        right_cell - 2.0 * left_cell + far_left,
        far_right - 2.0 * right_cell + left_cell,
    )
    face_value = (
        0.5 * (left_cell + right_cell)
        - 0.5 * courant * (right_cell - left_cell)
        - (1.0 - courant * courant) / 6.0 * curvature
    )
    flux_face = courant * face_value * face_weight
    difference = lax.slice_in_dim(flux_face, 1, cells + 1, axis=along_axis) - lax.slice_in_dim(
        flux_face, 0, cells, axis=along_axis
    )
    return piece_at(2, cells) - difference * cell_weight


def shards(spectra, u_wind, wind_dir, sea_mask):
    freq_local, band_rows, dir_count, lon_cells = spectra.shape
    comp_count = lax.axis_size("comp")
    block_rows = band_rows // comp_count
    comp_index = lax.axis_index("comp")
    mask_field = sea_mask.astype(jnp.float32)[None, :, None, :]
    masked = spectra * mask_field
    angles = (jnp.arange(dir_count, dtype=jnp.float32) * (2.0 * math.pi / dir_count)).reshape(
        1, 1, -1, 1
    )
    own_freq = frequency(comp_index * freq_local + jnp.arange(freq_local, dtype=jnp.int32))
    flattened = masked.reshape(freq_local, comp_count, block_rows, dir_count, lon_cells)
    growth = wind_growth(own_freq, angles, u_wind[None, :, None, :], wind_dir[None, :, None, :])
    wind_grown = masked * (1.0 + growth)
    change = nonlinear(
        lax.all_to_all(flattened, "comp", split_axis=1, concat_axis=0, tiled=True)[:, 0]
    )[:, None]
    increment = lax.all_to_all(change, "comp", split_axis=0, concat_axis=1, tiled=True)
    increment = increment.reshape(freq_local, band_rows, dir_count, lon_cells)
    padded = padded_2(wind_grown + increment, (("grid", 3),), 2)
    crossing = courant_x(own_freq, angles, jnp.arange(band_rows, dtype=jnp.int32), band_rows)
    swept_x = advect(padded, crossing, 1.0, 1.0, 3) * mask_field
    padded_rows = jnp.pad(swept_x, ((0, 0), (2, 2), (0, 0), (0, 0)))
    face_cos, cell_inverse = latitude_cos(band_rows)
    return advect(padded_rows, courant_y(own_freq, angles), face_cos, cell_inverse, 1) * mask_field


def solution(mesh):
    return jax.shard_map(
        shards,
        mesh=mesh,
        in_specs=(P("comp", None, None, "grid"), P(None, "grid"), P(None, "grid"), P(None, "grid")),
        out_specs=P("comp", None, None, "grid"),
        check_vma=False,
    )
```

profile of v0, /device:TPU:23, one launch (start us, length us, event | category | flops | bytes accessed | tf_op | source)
XLA Modules:
  0.0 293.2 jit_solution(14984558014049165961)
XLA Ops:
  0.0 0.8 convert_element_type.16
  0.8 5.6 %fusion.50 = f32[1,32,1,36,512]{4,2,3,0,1:T(1,128)} fusion(f32[32,512]{1,0:T(8,128)S(1)} %convert_element_type.16, f32[1,32,36,512]{3,1,2,0:T(8,128)} %param.4), kind=kLoop, calls=%fused_computation.69 | loop fusion | flops 589824 | bytes 4784128 | tf_op jit(solution)/shard_map/reshape | solution.py:167
  6.4 12.8 %all-to-all-start = ((f32[1,32,1,36,512]{4,2,3,0,1:T(1,128)}), f32[1,32,1,36,512]{4,2,3,0,1:T(1,128)S(1)}, u32[]{:S(2)}, u32[]{:S(2)}) async-start(f32[1,32,1,36,512]{4,2,3,0,1:T(1,128)} %fusion.50), calls=%async_computation | async-start | bytes 4718592 | tf_op jit(solution)/shard_map/all_to_all | solution.py:171
  19.3 52.8 %all-to-all-done = f32[1,32,1,36,512]{4,2,3,0,1:T(1,128)S(1)} async-done(((f32[1,32,1,36,512]{4,2,3,0,1:T(1,128)}), f32[1,32,1,36,512]{4,2,3,0,1:T(1,128)S(1)}, u32[]{:S(2)}, u32[]{:S(2)}) %all-to-all-start) | async-done | bytes 2359328 | tf_op jit(solution)/shard_map/all_to_all | solution.py:171
  72.1 2.6 fusion.32
  74.7 4.4 %fusion.14 = f32[32,512,36]{1,2,0:T(8,128)S(1)} fusion(f32[32,36,512]{2,0,1:T(8,128)S(1)} %fusion.32, f32[36]{0:T(128)S(1)} %iota_add_fusion), kind=kOutput, calls=%fused_computation.22 | convolution fusion | flops 254819520 | bytes 4718736 | tf_op jit(solution)/shard_map/jn,krnq->krjq/dot_general | solution.py:69
  79.1 4.4 %fusion.16 = f32[32,512,36]{1,2,0:T(8,128)S(1)} fusion(f32[32,36,512]{2,0,1:T(8,128)S(1)} %fusion.32, f32[36]{0:T(128)S(1)} %iota_add_fusion.2), kind=kOutput, calls=%fused_computation.24 | convolution fusion | flops 254819520 | bytes 4718736 | tf_op jit(solution)/shard_map/jn,krnq->krjq/dot_general | solution.py:69
  83.4 3.1 %fusion.34 = f32[32,36,512]{2,0,1:T(8,128)S(1)} fusion(f32[1,32,1,36,512]{4,2,3,0,1:T(1,128)S(1)} %all-to-all-done, f32[32]{0:T(128)S(1)} %iota_add_fusion.5), kind=kOutput, calls=%fused_computation.56 | convolution fusion | flops 226496512 | bytes 4718720 | tf_op jit(solution)/shard_map/km,mrjq->krjq/dot_general | solution.py:57
  86.6 4.4 %fusion.18 = f32[32,512,36]{1,2,0:T(8,128)S(1)} fusion(f32[32,36,512]{2,0,1:T(8,128)S(1)} %fusion.34, f32[36]{0:T(128)S(1)} %iota_add_fusion.1), kind=kOutput, calls=%fused_computation.26 | convolution fusion | flops 254819520 | bytes 4718736 | tf_op jit(solution)/shard_map/jn,krnq->krjq/dot_general | solution.py:68
  90.9 4.4 %fusion.20 = f32[32,512,36]{1,2,0:T(8,128)S(1)} fusion(f32[32,36,512]{2,0,1:T(8,128)S(1)} %fusion.34, f32[36]{0:T(128)S(1)} %iota_add_fusion.4), kind=kOutput, calls=%fused_computation.28 | convolution fusion | flops 254819520 | bytes 4718736 | tf_op jit(solution)/shard_map/jn,krnq->krjq/dot_general | solution.py:68
  95.3 6.9 %multiply_bitcast_fusion.1 = (f32[32,36,512]{2,0,1:T(8,128)S(1)}, f32[32,1,36,512]{3,0,2,1:T(8,128)S(1)}, f32[32,36,512]{2,0,1:T(8,128)S(1)}, f32[32,1,36,512]{3,0,2,1:T(8,128)S(1)}) fusion(f32[32,512,36]{1,2,0:T(8,128)S(1)} %fusion.16, f32[32,512,36]{1,2,0:T(8,128)S(1)} %fusion.20, f32[1,32,1,36,512]{4,2,3,0,1:T(1,128)S(1)} %all-to-all-done, ...), kind=kLoop, calls=%fused_computation.64 | loop fusion | flops 10616832 | bytes 21233664 | tf_op jit(solution)/shard_map/reshape.33
  102.2 4.3 %fusion.6 = f32[32,512,36]{1,2,0:T(8,128)S(1)} fusion(f32[32,36,512]{2,0,1:T(8,128)S(1)} %get-tuple-element.11, f32[36]{0:T(128)S(1)} %iota_add_fusion), kind=kOutput, calls=%fused_computation.14 | convolution fusion | flops 254819520 | bytes 4718736 | tf_op jit(solution)/shard_map/jn,krjq->krnq/dot_general | solution.py:78
  106.6 4.3 %fusion.8 = f32[32,512,36]{1,2,0:T(8,128)S(1)} fusion(f32[32,36,512]{2,0,1:T(8,128)S(1)} %get-tuple-element.11, f32[36]{0:T(128)S(1)} %iota_add_fusion.1), kind=kOutput, calls=%fused_computation.16 | convolution fusion | flops 254819520 | bytes 4718736 | tf_op jit(solution)/shard_map/jn,krjq->krnq/dot_general | solution.py:75
  110.9 4.8 %add_bitcast_fusion = f32[32,36,512]{2,1,0:T(8,128)S(1)} fusion(f32[32,512,36]{1,2,0:T(8,128)S(1)} %fusion.6, f32[32,36,512]{2,0,1:T(8,128)S(1)} %get-tuple-element.5, f32[36]{0:T(128)S(1)} %iota_add_fusion.2), kind=kOutput, calls=%fused_computation.12 | convolution fusion | flops 255409344 | bytes 7078032 | tf_op jit(solution)/shard_map/jn,krjq->krnq/dot_general | solution.py:78
  115.7 3.4 %fusion.36 = f32[32,36,512]{2,0,1:T(8,128)S(1)} fusion(f32[32,36,512]{2,1,0:T(8,128)S(1)} %add_bitcast_fusion, f32[32]{0:T(128)S(1)} %iota_add_fusion.3), kind=kOutput, calls=%fused_computation.58 | convolution fusion | flops 226496512 | bytes 4718720 | tf_op jit(solution)/shard_map/km,krjq->mrjq/dot_general | solution.py:84
  119.1 4.6 %add_bitcast_fusion.1 = f32[32,36,512]{2,1,0:T(8,128)S(1)} fusion(f32[32,512,36]{1,2,0:T(8,128)S(1)} %fusion.8, f32[32,36,512]{2,0,1:T(8,128)S(1)} %get-tuple-element.5, f32[36]{0:T(128)S(1)} %iota_add_fusion.4), kind=kOutput, calls=%fused_computation.13 | convolution fusion | flops 255409344 | bytes 7078032 | tf_op jit(solution)/shard_map/jn,krjq->krnq/dot_general | solution.py:75
  123.7 4.4 %fusion.25 = f32[32,1,1,36,512]{4,0,3,2,1:T(8,128)S(1)} fusion(f32[32,36,512]{2,0,1:T(8,128)S(1)} %fusion.36, f32[32,1,36,512]{3,0,2,1:T(8,128)S(1)} %get-tuple-element.12, f32[32,1,36,512]{3,0,2,1:T(8,128)S(1)} %get-tuple-element.6, f32[32,36,512]{2,1,0:T(8,128)S(1)} %add_bitcast_fusion.1, f32[32]{0:T(128)S(1)} %iota_add_fusion.5), kind=kOutput, calls=%fused_computation.38 | convolution fusion | flops 230035456 | bytes 11796608 | tf_op jit(solution)/shard_map/km,krjq->mrjq/dot_general | solution.py:81
  128.1 3.8 %copy.100 = f32[32,1,1,36,512]{4,2,3,1,0:T(1,128)} copy(f32[32,1,1,36,512]{4,0,3,2,1:T(8,128)S(1)} %fusion.25) | data formatting | bytes 4718592 | tf_op jit(solution)/shard_map/broadcast_in_dim | solution.py:170
  131.9 12.4 %all-to-all-start.1 = ((f32[32,1,1,36,512]{4,2,3,1,0:T(1,128)}), f32[32,1,1,36,512]{4,2,3,1,0:T(1,128)S(1)}, u32[]{:S(2)}, u32[]{:S(2)}) async-start(f32[32,1,1,36,512]{4,2,3,1,0:T(1,128)} %copy.100), calls=%async_computation.1 | async-start | bytes 4718592 | tf_op jit(solution)/shard_map/all_to_all | solution.py:173
  144.4 0.6 multiply_cosine_fusion
  145.0 0.6 broadcast_compare_fusion.1
  145.7 0.6 subtract_multiply_fusion.1
  146.3 0.6 multiply_multiply_fusion.2
  146.9 0.7 broadcast_compare_fusion
  147.6 0.7 broadcast_divide_fusion.1
  148.3 0.0 copy-done.3
  148.3 0.0 copy-done.4
  148.3 0.2 fusion.208
  148.5 49.7 %all-to-all-done.1 = f32[32,1,1,36,512]{4,2,3,1,0:T(1,128)S(1)} async-done(((f32[32,1,1,36,512]{4,2,3,1,0:T(1,128)}), f32[32,1,1,36,512]{4,2,3,1,0:T(1,128)S(1)}, u32[]{:S(2)}, u32[]{:S(2)}) %all-to-all-start.1) | async-done | bytes 2359328 | tf_op jit(solution)/shard_map/all_to_all | solution.py:173
  198.2 1.4 copy-done
  199.6 0.0 copy-done.1
  199.6 8.7 %bitcast_add_fusion = f32[1,32,36,512]{3,0,2,1:T(1,128)S(1)} fusion(f32[32,1,1,36,512]{4,2,3,1,0:T(1,128)} %copy-done, f32[32,512]{1,0:T(8,128)S(1)} %get-tuple-element.14, f32[32,512]{1,0:T(8,128)S(1)} %get-tuple-element.13, f32[32,512]{1,0:T(8,128)S(1)} %get-tuple-element.18, f32[]{:T(128)S(6)} %mul.452, f32[36]{0:T(128)S(1)} %get-tuple-element.19, ...), kind=kLoop, calls=%fused_computation.36 | loop fusion | flops 6488064 | bytes 7340324 | tf_op jit(solution)/shard_map/add | solution.py:175
  208.3 1.6 fusion.207
  209.9 1.1 copy.101
  211.0 11.9 %collective-permute-start = (f32[1,32,36,2]{2,1,3,0:T(8,128)}, f32[1,32,36,2]{2,1,3,0:T(8,128)S(1)}, u32[]{:S(2)}, u32[]{:S(2)}) collective-permute-start(f32[1,32,36,2]{2,1,3,0:T(8,128)} %copy.101), channel_id=1, source_target_pairs={{0,32},{32,64},{64,96},{96,128},{128,160},{160,192},{192,224},{224... | collective-permute-start | bytes 27656 | tf_op jit(solution)/shard_map/ppermute | solution.py:35
  222.9 0.5 copy.103
  223.3 1.9 collective-permute-start.1
  225.3 0.6 cosine_divide_fusion
  225.9 0.0 collective-permute-done
  225.9 0.6 copy.102
  226.5 8.2 %collective-permute-done.1 = f32[1,32,36,2]{2,1,3,0:T(8,128)} collective-permute-done((f32[1,32,36,2]{2,1,3,0:T(8,128)S(1)}, f32[1,32,36,2]{2,1,3,0:T(8,128)}, u32[]{:S(2)}, u32[]{:S(2)}) %collective-permute-start.1) | collective-permute-done | bytes 9248 | tf_op jit(solution)/shard_map/ppermute | solution.py:38
  234.7 1.2 copy.104
  235.9 0.0 copy-start.2
  235.9 33.6 %fusion.5 = f32[1,32,36,513]{3,0,2,1:T(1,128)S(1)} fusion(f32[1,32,36,2]{3,0,2,1:T(1,128)S(1)} %copy.104, f32[1,32,36,512]{3,0,2,1:T(1,128)S(1)} %bitcast_add_fusion, f32[1,32,36,2]{3,0,2,1:T(1,128)S(1)} %copy.102, pred[32,36]{1,0:T(8,128)(4,1)} %broadcast_compare_fusion, f32[32,36]{1,0:T(8,128)} %get-tuple-element.17, f32[32,36]{1,0:T(8,128)} %get-tuple-element.16, ...), kind=kLoop, calls=%fused_computation.11 | loop fusion | flops 11228544 | bytes 4756608 | tf_op jit(solution)/shard_map/mul | solution.py:149
  269.6 5.3 %fusion.40 = f32[1,32,36,512]{3,0,2,1:T(1,128)S(1)} fusion(f32[1,32,36,512]{3,0,2,1:T(1,128)S(1)} %bitcast_add_fusion, f32[1,32,36,513]{3,0,2,1:T(1,128)S(1)} %fusion.5, f32[32,512]{1,0:T(8,128)S(1)} %copy-done.2), kind=kLoop, calls=%fused_computation.65 | loop fusion | flops 1769472 | bytes 9502720 | tf_op jit(solution)/shard_map/mul | solution.py:177
  275.0 11.4 %multiply_multiply_fusion = f32[1,33,36,512]{3,0,2,1:T(1,128)S(1)} fusion(pred[36]{0:T(512)(128)(4,1)S(1)} %copy-done.6, f32[1,32,36,512]{3,0,2,1:T(1,128)S(1)} %fusion.40, f32[33]{0:T(128)S(1)} %copy-done.5, f32[36]{0:T(128)S(1)} %copy-done.7, f32[36]{0:T(128)S(1)} %copy-done.8, f32[36]{0:T(128)S(1)} %copy-done.9), kind=kLoop, calls=%fused_computation.30 | loop fusion | flops 9732096 | bytes 4792920 | tf_op jit(solution)/shard_map/mul | solution.py:149
  286.4 4.5 %fusion.41 = f32[1,32,36,512]{3,0,2,1:T(1,128)S(1)} fusion(f32[1,32,36,512]{3,0,2,1:T(1,128)S(1)} %fusion.40, f32[1,33,36,512]{3,0,2,1:T(1,128)S(1)} %multiply_multiply_fusion, f32[32]{0:T(128)S(1)} %copy-done.10, f32[32,512]{1,0:T(8,128)S(1)} %copy-done.2), kind=kLoop, calls=%fused_computation.66 | loop fusion | flops 2359296 | bytes 9502848 | tf_op jit(solution)/shard_map/mul | solution.py:180
  290.9 2.1 copy.105
  (25 shorter events, 0.2 us)
Async XLA Ops:
  0.8 198.8 %copy-start.1 = (f32[32,512]{1,0:T(8,128)}, f32[32,512]{1,0:T(8,128)S(1)}, u32[]{:S(2)}) copy-start(f32[32,512]{1,0:T(8,128)S(1)} %convert_element_type.16) | copy-start | bytes 196612
  6.4 65.7 %all-to-all-start = ((f32[1,32,1,36,512]{4,2,3,0,1:T(1,128)}), f32[1,32,1,36,512]{4,2,3,0,1:T(1,128)S(1)}, u32[]{:S(2)}, u32[]{:S(2)}) async-start(f32[1,32,1,36,512]{4,2,3,0,1:T(1,128)} %fusion.50), calls=%async_computation | async-start | bytes 4718592 | tf_op jit(solution)/shard_map/all_to_all | solution.py:171
  131.9 16.4 %copy-start.3 = (f32[32,512]{1,0:T(8,128)S(1)}, f32[32,512]{1,0:T(8,128)}, u32[]{:S(2)}) copy-start(f32[32,512]{1,0:T(8,128)} %param.6) | copy-start | bytes 196612
  131.9 16.4 %copy-start.4 = (f32[32,512]{1,0:T(8,128)S(1)}, f32[32,512]{1,0:T(8,128)}, u32[]{:S(2)}) copy-start(f32[32,512]{1,0:T(8,128)} %param.5) | copy-start | bytes 196612
  131.9 66.3 %all-to-all-start.1 = ((f32[32,1,1,36,512]{4,2,3,1,0:T(1,128)}), f32[32,1,1,36,512]{4,2,3,1,0:T(1,128)S(1)}, u32[]{:S(2)}, u32[]{:S(2)}) async-start(f32[32,1,1,36,512]{4,2,3,1,0:T(1,128)} %copy.100), calls=%async_computation.1 | async-start | bytes 4718592 | tf_op jit(solution)/shard_map/all_to_all | solution.py:173
  198.2 1.4 copy-start
  211.0 14.9 %collective-permute-start = (f32[1,32,36,2]{2,1,3,0:T(8,128)}, f32[1,32,36,2]{2,1,3,0:T(8,128)S(1)}, u32[]{:S(2)}, u32[]{:S(2)}) collective-permute-start(f32[1,32,36,2]{2,1,3,0:T(8,128)} %copy.101), channel_id=1, source_target_pairs={{0,32},{32,64},{64,96},{96,128},{128,160},{160,192},{192,224},{224... | collective-permute-start | bytes 27656 | tf_op jit(solution)/shard_map/ppermute | solution.py:35
  223.3 11.4 %collective-permute-start.1 = (f32[1,32,36,2]{2,1,3,0:T(8,128)S(1)}, f32[1,32,36,2]{2,1,3,0:T(8,128)}, u32[]{:S(2)}, u32[]{:S(2)}) collective-permute-start(f32[1,32,36,2]{2,1,3,0:T(8,128)S(1)} %copy.103), channel_id=1, source_target_pairs={{32,0},{64,32},{96,64},{128,96},{160,128},{192,160},{224,192},{256... | collective-permute-start | bytes 27656 | tf_op jit(solution)/shard_map/ppermute | solution.py:38
  235.9 33.6 %copy-start.2 = (f32[32,512]{1,0:T(8,128)S(1)}, f32[32,512]{1,0:T(8,128)}, u32[]{:S(2)}) copy-start(f32[32,512]{1,0:T(8,128)} %copy-done.1) | copy-start | bytes 196612
  269.5 5.4 %copy-start.5 = (f32[33]{0:T(128)S(1)}, f32[33]{0:T(128)}, u32[]{:S(2)}) copy-start(f32[33]{0:T(128)} %multiply_cosine_fusion) | copy-start | bytes 400
  269.5 5.4 %copy-start.6 = (pred[36]{0:T(512)(128)(4,1)S(1)}, pred[36]{0:T(512)(128)(4,1)}, u32[]{:S(2)}) copy-start(pred[36]{0:T(512)(128)(4,1)} %broadcast_compare_fusion.1) | copy-start | bytes 112
  269.6 5.4 %copy-start.7 = (f32[36]{0:T(128)S(1)}, f32[36]{0:T(128)}, u32[]{:S(2)}) copy-start(f32[36]{0:T(128)} %get-tuple-element.21) | copy-start | bytes 436
  269.6 5.4 %copy-start.8 = (f32[36]{0:T(128)S(1)}, f32[36]{0:T(128)}, u32[]{:S(2)}) copy-start(f32[36]{0:T(128)} %get-tuple-element.23) | copy-start | bytes 436
  269.6 5.4 %copy-start.9 = (f32[36]{0:T(128)S(1)}, f32[36]{0:T(128)}, u32[]{:S(2)}) copy-start(f32[36]{0:T(128)} %get-tuple-element.24) | copy-start | bytes 436
  275.0 11.4 %copy-start.10 = (f32[32]{0:T(128)S(1)}, f32[32]{0:T(128)}, u32[]{:S(2)}) copy-start(f32[32]{0:T(128)} %cosine_divide_fusion) | copy-start | bytes 388
where the time goes:
time: 297 us; the launch traced here: 293 us
  waiting for transfers between devices  111 us (37%)
  other arithmetic  81.7 us (28%)
  matrix products  48.9 us (16%)
  starting transfers between devices  38.9 us (13%)
  local copies, waits for them, and re-layouts  12.3 us (4%)
    all_to_all x1, waiting for transfers between devices, shards(): lax.all_to_all(flattened, 'comp', split_axis=1, concat_axis=0, tiled=True)  52.8 us
    all_to_all x1, waiting for transfers between devices, shards(): lax.all_to_all(change, 'comp', split_axis=0, concat_axis=1, tiled=True)  49.7 us
    mul x2, other arithmetic, advect(): flux_face = courant * face_value * face_weight  45 us
    all_to_all x1, starting transfers between devices, shards(): lax.all_to_all(flattened, 'comp', split_axis=1, concat_axis=0, tiled=True)  12.8 us
    all_to_all x1, starting transfers between devices, shards(): lax.all_to_all(change, 'comp', split_axis=0, concat_axis=1, tiled=True)  12.4 us
    ppermute x1, starting transfers between devices, padded_2(): lax.ppermute(lax.slice_in_dim(block, block.shape[dim] - width, None, axis...  11.9 us
    dot_general x2, matrix products, nonlinear(): jnp.einsum('jn,krjq->krnq', dir_lower, interaction, precision=HIGHEST)  9.12 us
    dot_general x2, matrix products, nonlinear(): jnp.einsum('jn,krjq->krnq', dir_upper, interaction, precision=HIGHEST)  8.91 us
  transfers between devices with their start and end apart: 4, of which 3 were waited for; matrix products, arithmetic and copies ran while one was open for 2% of the time, Pallas kernels for 0%

commit v1 on v0

v1 whole, which is shorter than its diff:
```python
import math

import numpy as np

import jax
import jax.numpy as jnp
from jax import lax
from jax.experimental import pallas as pl
from jax.experimental.pallas import tpu as pltpu
from jax.sharding import PartitionSpec as P

MESH = pl.DeviceIdType.MESH
NK, NTH, LAT = 32, 36, 32
GRAVITY = 9.81
LAMBDA = 0.25
WIND = 0.0003125 * 120.0
ADVECT_STEP = 220.0
EARTH_RADIUS = 6371000.0
BAND_CENTRE = 30.0
CELL_DEGREES = 0.05
CELL_RADIANS = CELL_DEGREES * math.pi / 180.0
SHIFT_UP = math.log(1.0 + LAMBDA) / math.log(1.1)
SHIFT_DOWN = math.log(1.0 - LAMBDA) / math.log(1.1)
NEAR = 11.48 * NTH / 360.0
FAR = 33.56 * NTH / 360.0
U1 = SHIFT_UP - 2.0
U0 = 1.0 - U1
D1W = -SHIFT_DOWN - 3.0
D0W = 1.0 - D1W
N1 = NEAR - 1.0
N0 = 1.0 - N1
F1 = FAR - 3.0
F0 = 1.0 - F1
W_UP = 0.1 / (1.0 + LAMBDA) ** 4
W_DOWN = 0.1 / (1.0 - LAMBDA) ** 4
W_CROSS = 0.2 / (1.0 - LAMBDA * LAMBDA) ** 4

ORDER = (0, 3, 1, 2)
LANES = 128
JB = 4
PAD = 4


def tables():
    t = np.zeros((8, 128), np.float64)
    th = 2.0 * np.pi * np.arange(NTH) / NTH
    t[0, :NTH] = np.cos(th)
    t[1, :NTH] = np.sin(th)
    f = 0.04 * 1.1 ** np.arange(NK)
    w = 2.0 * np.pi * f
    t[2, :NK] = WIND * w
    t[3, :NK] = w / GRAVITY
    t[4, :NK] = GRAVITY / (2.0 * w) * ADVECT_STEP / (EARTH_RADIUS * CELL_RADIANS)
    i = np.arange(LAT)
    cell = np.cos(np.radians(BAND_CENTRE + (i - (LAT - 1) / 2.0) * CELL_DEGREES))
    upper = np.cos(np.radians(BAND_CENTRE + (i + 1 - LAT / 2.0) * CELL_DEGREES))
    lower = np.cos(np.radians(BAND_CENTRE + (i - LAT / 2.0) * CELL_DEGREES))
    t[5, :LAT] = upper / cell
    t[6, :LAT] = lower / cell
    return t.astype(np.float32)


def kernel(
    tab, x_hbm, uw, wd, mk, o_hbm,
    xbuf, obuf, sbuf, ebuf, tbuf, above, below, incr, ibuf, post,
    eux, edx, d1x, d2x, bus, bds, cen, swept, ybuf, taps, rowinv,
    pack_l, pack_r, halo_l, halo_r,
    load_s, store_s, zin_s, zin_r, hal_s, hal_r, bak_s, bak_r, zout_s, zout_r, lon_s, lon_r,
):
    f32 = jnp.float32
    me = lax.axis_index("comp")
    g = lax.axis_index("grid")
    y, z = me // 4, lax.rem(me, 4)
    y_up = lax.rem(y + 1, 8) * 4 + z
    y_dn = lax.rem(y + 7, 8) * 4 + z
    g_right, g_left = lax.rem(g + 1, 16), lax.rem(g + 15, 16)
    has_lo = jnp.where(y > 0, 1.0, 0.0).astype(f32)
    has_hi = jnp.where(y < 7, 1.0, 0.0).astype(f32)
    has_left = jnp.where(g > 0, 1.0, 0.0).astype(f32)
    has_right = jnp.where(g < 15, 1.0, 0.0).astype(f32)

    def zpeer(dz):
        return lax.rem(z + dz, 4)

    def zfrom(dz):
        return lax.rem(z + 4 - dz, 4)

    def load(i):
        return pltpu.make_async_copy(
            x_hbm.at[0, :, :, pl.ds(ORDER[i] * LANES, LANES)], xbuf.at[i], load_s.at[i]
        )

    def store(i):
        return pltpu.make_async_copy(
            obuf.at[i], o_hbm.at[0, :, :, pl.ds(ORDER[i] * LANES, LANES)], store_s.at[i]
        )

    def remote(src, dst, ss, rs, **to):
        return pltpu.make_async_remote_copy(
            src_ref=src, dst_ref=dst, send_sem=ss, recv_sem=rs, device_id=to, device_id_type=MESH
        )

    def zin(i, dz):
        p = zpeer(dz)
        k = i * 4 + dz
        return remote(sbuf.at[i, p], ebuf.at[i, 4 + z], zin_s.at[k], zin_r.at[k], comp=y * 4 + p)

    def hal_up(i, f):
        k = i * 8 + f
        return remote(ebuf.at[i, 4 + f], ebuf.at[i, f], hal_s.at[k], hal_r.at[k], comp=y_up)

    def hal_dn(i, f):
        k = i * 8 + 4 + f
        return remote(ebuf.at[i, 4 + f], ebuf.at[i, 8 + f], hal_s.at[k], hal_r.at[k], comp=y_dn)

    def bak_dn(i, m):
        k = i * 8 + m
        return remote(tbuf.at[i, m], above.at[i, m], bak_s.at[k], bak_r.at[k], comp=y_dn)

    def bak_up(i, m):
        k = i * 8 + 4 + m
        return remote(tbuf.at[i, 8 + m], below.at[i, m], bak_s.at[k], bak_r.at[k], comp=y_up)

    def zout(i, dz):
        p = zpeer(dz)
        k = i * 4 + dz
        return remote(incr.at[i, p], ibuf.at[i, z], zout_s.at[k], zout_r.at[k], comp=y * 4 + p)

    def lon_to_right():
        return remote(pack_r, halo_l, lon_s.at[0], lon_r.at[0], grid=g_right)

    def lon_to_left():
        return remote(pack_l, halo_r, lon_s.at[1], lon_r.at[1], grid=g_left)

    for i in range(4):
        load(i).start()

    barrier = pltpu.get_barrier_semaphore()
    for dz in (1, 2, 3):
        pl.semaphore_signal(barrier, inc=1, device_id={"comp": y * 4 + zpeer(dz)}, device_id_type=MESH)
    pl.semaphore_signal(barrier, inc=1, device_id={"comp": y_up}, device_id_type=MESH)
    pl.semaphore_signal(barrier, inc=1, device_id={"comp": y_dn}, device_id_type=MESH)
    pl.semaphore_signal(barrier, inc=1, device_id={"grid": g_right}, device_id_type=MESH)
    pl.semaphore_signal(barrier, inc=1, device_id={"grid": g_left}, device_id_type=MESH)

    def lanes(i):
        return slice(ORDER[i] * LANES, (ORDER[i] + 1) * LANES)

    def rows8(rg):
        return pl.ds(pl.multiple_of(rg * 8, 8), 8)

    def prepare(i):
        load(i).wait()
        for dz in (2, 1, 3, 0):
            rg = zpeer(dz)
            piece = jnp.swapaxes(xbuf[i, rows8(rg)], 0, 1)
            piece = piece * mk[rows8(rg), lanes(i)].astype(f32)[None]
            sbuf[i, rg] = piece
            if dz == 0:
                ebuf[i, 4 + z] = piece
            else:
                if i == 0 and dz == 2:
                    pl.semaphore_wait(barrier, 7)
                zin(i, dz).start()

    wind_w = tab[2, me]
    inv_cel = tab[3, me]
    courant = tab[4, me]

    def grow(i):
        for rg in range(4):
            speed = uw[rg * 8 : rg * 8 + 8, lanes(i)] * inv_cel
            head = wd[rg * 8 : rg * 8 + 8, lanes(i)]
            along, across = speed * jnp.cos(head), speed * jnp.sin(head)

            @pl.loop(0, NTH, unroll=4)
            def _(j):
                growth = wind_w * jnp.maximum(0.0, tab[0, j] * along + tab[1, j] * across - 1.0)
                post[i, rg, j] = sbuf[i, rg, j] * (1.0 + growth)

    def constants():
        row = lax.broadcasted_iota(jnp.int32, (LAT, LANES), 0).astype(f32)
        lat = BAND_CENTRE + (row - (LAT - 1) / 2.0) * CELL_DEGREES
        rowinv[...] = 1.0 / jnp.cos(lat * (math.pi / 180.0))
        j = lax.broadcasted_iota(jnp.int32, (NTH, LANES), 0).astype(f32)
        c = courant * jnp.sin(j * (2.0 * math.pi / NTH))
        q = (1.0 - c * c) / 6.0
        pos = c >= 0.0
        taps[0] = c * jnp.where(pos, -q, 0.0)
        taps[1] = c * (0.5 + 0.5 * c + jnp.where(pos, 2.0 * q, -q))
        taps[2] = c * (0.5 - 0.5 * c + jnp.where(pos, -q, 2.0 * q))
        taps[3] = c * jnp.where(pos, 0.0, -q)
        for i in range(4):
            below[i, 3] = jnp.zeros((NTH, 8, LANES), f32)
        ybuf[0:2] = jnp.zeros((2, NTH, LANES), f32)
        ybuf[LAT + 2 : LAT + 4] = jnp.zeros((2, NTH, LANES), f32)

    def forward(i):
        for dz in range(4):
            f = zfrom(dz)
            if dz:
                zin(i, dz).wait_recv()
            hal_up(i, f).start()

            @pl.when(f < 3)
            def _():
                hal_dn(i, f).start()

    def interact(i):
        for f in range(4):
            hal_up(i, f).wait_recv()
        for f in range(3):
            hal_dn(i, f).wait_recv()

        @pl.loop(0, 4)
        def _(k):
            lo_a = jnp.where(k < 4, has_lo, 1.0) * D1W
            lo_b = jnp.where(k < 3, has_lo, 1.0) * D0W
            hi_a = jnp.where(k >= 2, has_hi, 1.0) * U0
            hi_b = jnp.where(k >= 1, has_hi, 1.0) * U1

            @pl.loop(0, NTH // JB)
            def _(b):
                at = pl.ds(b * JB, JB)
                to = pl.ds(b * JB + PAD, JB)
                eux[to] = hi_a * ebuf[i, k + 6, at] + hi_b * ebuf[i, k + 7, at]
                edx[to] = lo_b * ebuf[i, k + 1, at] + lo_a * ebuf[i, k, at]

            for ref in (eux, edx):
                ref[0:PAD] = ref[NTH : NTH + PAD]
                ref[NTH + PAD : NTH + 2 * PAD] = ref[PAD : 2 * PAD]

            @pl.loop(0, NTH // JB)
            def _(b):
                def eu(o):
                    return eux[pl.ds(b * JB + PAD + o, JB)]

                def ed(o):
                    return edx[pl.ds(b * JB + PAD + o, JB)]

                e = ebuf[i, k + 4, pl.ds(b * JB, JB)]

                def delta(plus, minus):
                    return e * (e * (W_UP * plus + W_DOWN * minus) - W_CROSS * plus * minus)

                to = pl.ds(b * JB + PAD, JB)
                d1x[to] = delta(N0 * eu(1) + N1 * eu(2), F0 * ed(-3) + F1 * ed(-4))
                d2x[to] = delta(N0 * eu(-1) + N1 * eu(-2), F0 * ed(3) + F1 * ed(4))

            for ref in (d1x, d2x):
                ref[0:PAD] = ref[NTH : NTH + PAD]
                ref[NTH + PAD : NTH + 2 * PAD] = ref[PAD : 2 * PAD]

            @pl.loop(0, NTH // JB)
            def _(b):
                def a1(o):
                    return d1x[pl.ds(b * JB + PAD + o, JB)]

                def a2(o):
                    return d2x[pl.ds(b * JB + PAD + o, JB)]

                at = pl.ds(b * JB, JB)
                bus[k, at] = N0 * (a1(-1) + a2(1)) + N1 * (a1(-2) + a2(2))
                bds[k, at] = F0 * (a1(3) + a2(-3)) + F1 * (a1(4) + a2(-4))
                cen[k, at] = -2.0 * (a1(0) + a2(0))

        @pl.loop(0, NTH)
        def _(j):
            bd = [bds[k, j] for k in range(4)]
            bu = [bus[k, j] for k in range(4)]
            tbuf[i, 0, j] = D1W * bd[0]
            tbuf[i, 1, j] = D0W * bd[0] + D1W * bd[1]
            tbuf[i, 2, j] = D0W * bd[1] + D1W * bd[2]
            tbuf[i, 3, j] = D0W * bd[2] + D1W * bd[3]
            tbuf[i, 4, j] = cen[0, j] + D0W * bd[3]
            tbuf[i, 5, j] = cen[1, j]
            tbuf[i, 6, j] = cen[2, j] + U0 * bu[0]
            tbuf[i, 7, j] = cen[3, j] + U1 * bu[0] + U0 * bu[1]
            tbuf[i, 8, j] = U1 * bu[1] + U0 * bu[2]
            tbuf[i, 9, j] = U1 * bu[2] + U0 * bu[3]
            tbuf[i, 10, j] = U1 * bu[3]

        for m in range(4):
            bak_dn(i, m).start()
            if m < 3:
                bak_up(i, m).start()

    def gather(i):
        for dz in (1, 2, 3, 0):
            m = zpeer(dz)
            bak_dn(i, m).wait_recv()

            @pl.when(m < 3)
            def _():
                bak_up(i, m).wait_recv()

            total = tbuf[i, 4 + m] + has_hi * above[i, m] + has_lo * below[i, m]
            if dz == 0:
                ibuf[i, z] = total
            else:
                incr[i, m] = total
                zout(i, dz).start()

    def finish(i):
        for dz in (1, 2, 3):
            zout(i, dz).wait_recv()

        @pl.loop(0, NTH // JB)
        def _(b):
            at = pl.ds(b * JB, JB)
            for rg in range(4):
                post[i, rg, at] = post[i, rg, at] + ibuf[i, rg, at]

    lane = lax.broadcasted_iota(jnp.int32, (8, LANES), 1)

    def edges():
        first, last = ORDER.index(0), ORDER.index(3)
        for rg in range(4):

            def step(j, acc):
                a, b = acc
                here = (lane == 2 * j) | (lane == 2 * j + 1)
                a = jnp.where(here, pltpu.roll(post[first, rg, j], 2 * j, 1), a)
                b = jnp.where(here, pltpu.roll(post[last, rg, j], 2 * j + 2, 1), b)
                return a, b

            zero = jnp.zeros((8, LANES), f32)
            a, b = lax.fori_loop(0, NTH, step, (zero, zero), unroll=4)
            pack_l[rg] = a
            pack_r[rg] = b
        lon_to_right().start()
        lon_to_left().start()

    def sweep_x(chunks, rg, j, positive, edge_l, edge_r):
        c = (courant * tab[0, j]) * rowinv[rg * 8 : rg * 8 + 8]
        q = (1.0 - c * c) * (1.0 / 6.0)
        one = -q
        if positive:
            mid = 0.5 + 0.5 * c + 2.0 * q
            far = 0.5 - 0.5 * c - q
        else:
            mid = 0.5 - 0.5 * c + 2.0 * q
            far = 0.5 + 0.5 * c - q
        sign = c if positive else -c
        k_next, k_here = sign * far, sign * (mid - far)
        k_back, k_back2 = sign * (one - mid), sign * one
        k_here = 1.0 - k_here
        for col in chunks:
            v = post[ORDER.index(col), rg, j]
            if col == 0:
                vl = edge_l
            else:
                vl = post[ORDER.index(col - 1), rg, j]
            if col == 3:
                vr = edge_r
            else:
                vr = post[ORDER.index(col + 1), rg, j]
            if positive:
                nxt = pltpu.roll(jnp.where(lane == 0, vr, v), LANES - 1, 1)
                back = pltpu.roll(jnp.where(lane == LANES - 1, vl, v), 1, 1)
                back2 = pltpu.roll(jnp.where(lane >= LANES - 2, vl, v), 2, 1)
            else:
                nxt = pltpu.roll(jnp.where(lane == LANES - 1, vl, v), 1, 1)
                back = pltpu.roll(jnp.where(lane == 0, vr, v), LANES - 1, 1)
                back2 = pltpu.roll(jnp.where(lane < 2, vr, v), LANES - 2, 1)
            out = k_here * v - (k_next * nxt + k_back * back - k_back2 * back2)
            swept[ORDER.index(col), rg, j] = out

    def propagate(chunks):
        for rg in range(4):

            @pl.loop(0, NTH // 2)
            def _(t):
                for positive in (True, False):
                    j = lax.rem(t + 27, NTH) if positive else t + 9
                    edge_l = edge_r = None
                    if 0 in chunks:
                        edge_l = has_left * pltpu.roll(halo_l[rg], 126 - 2 * j, 1)
                    if 3 in chunks:
                        edge_r = has_right * pltpu.roll(halo_r[rg], LANES - 2 * j, 1)
                    sweep_x(chunks, rg, j, positive, edge_l, edge_r)

        for col in chunks:
            i = ORDER.index(col)
            for rg in range(4):
                sea = mk[rg * 8 : rg * 8 + 8, lanes(i)].astype(f32)
                ybuf[2 + rg * 8 : 10 + rg * 8] = jnp.swapaxes(swept[i, rg] * sea[None], 0, 1)

            def flux(r):
                return (
                    taps[0] * ybuf[r + 1] + taps[1] * ybuf[r + 2]
                    + taps[2] * ybuf[r + 3] + taps[3] * ybuf[r + 4]
                )

            def rows(block, under):
                sea = mk[rows8(block), lanes(i)].astype(f32)
                for s in range(8):
                    r = block * 8 + s
                    over = flux(r)
                    out = ybuf[r + 2] - (tab[5, r] * over - tab[6, r] * under)
                    obuf[i, r] = out * sea[s : s + 1]
                    under = over
                return under

            first = taps[2] * ybuf[2] + taps[3] * ybuf[3]
            lax.fori_loop(0, LAT // 8, rows, first)
            store(i).start()

    prepare(0)
    prepare(1)
    constants()
    grow(0)
    forward(0)
    prepare(2)
    grow(1)
    forward(1)
    prepare(3)
    interact(0)
    grow(2)
    forward(2)
    interact(1)
    grow(3)
    gather(0)
    forward(3)
    interact(2)
    gather(1)
    interact(3)
    finish(0)
    gather(2)
    finish(1)
    edges()
    gather(3)
    finish(2)
    lon_to_right().wait_recv()
    lon_to_left().wait_recv()
    propagate((0,))
    finish(3)
    propagate((1, 2, 3))

    for i in range(4):
        for dz in (1, 2, 3):
            zin(i, dz).wait_send()
            zout(i, dz).wait_send()
        for f in range(4):
            hal_up(i, f).wait_send()
            bak_dn(i, f).wait_send()
        for f in range(3):
            hal_dn(i, f).wait_send()
            bak_up(i, f).wait_send()
        store(i).wait()
    lon_to_right().wait_send()
    lon_to_left().wait_send()


def shards(spectra, u_wind, wind_dir, sea_mask):
    f32 = jnp.float32
    tile = (NTH, 8, LANES)
    vmem, dma = pltpu.VMEM, pltpu.SemaphoreType.DMA
    inner = pl.BlockSpec(memory_space=pltpu.VMEM)
    return pl.pallas_call(
        kernel,
        out_shape=jax.ShapeDtypeStruct(spectra.shape, f32),
        in_specs=[
            pl.BlockSpec(memory_space=pltpu.SMEM),
            pl.BlockSpec(memory_space=pl.ANY),
            inner, inner, inner,
        ],
        out_specs=pl.BlockSpec(memory_space=pl.ANY),
        scratch_shapes=[
            vmem((4, LAT, NTH, LANES), f32),
            vmem((4, LAT, NTH, LANES), f32),
            vmem((4, 4) + tile, f32),
            vmem((4, 11) + tile, f32),
            vmem((4, 11) + tile, f32),
            vmem((4, 4) + tile, f32),
            vmem((4, 4) + tile, f32),
            vmem((4, 4) + tile, f32),
            vmem((4, 4) + tile, f32),
            vmem((4, 4) + tile, f32),
            vmem((NTH + 2 * PAD, 8, LANES), f32),
            vmem((NTH + 2 * PAD, 8, LANES), f32),
            vmem((NTH + 2 * PAD, 8, LANES), f32),
            vmem((NTH + 2 * PAD, 8, LANES), f32),
            vmem((4,) + tile, f32),
            vmem((4,) + tile, f32),
            vmem((4,) + tile, f32),
            vmem((4, 4) + tile, f32),
            vmem((LAT + 4, NTH, LANES), f32),
            vmem((4, NTH, LANES), f32),
            vmem((LAT, LANES), f32),
            vmem((4, 8, LANES), f32),
            vmem((4, 8, LANES), f32),
            vmem((4, 8, LANES), f32),
            vmem((4, 8, LANES), f32),
            dma((4,)), dma((4,)),
            dma((16,)), dma((16,)),
            dma((32,)), dma((32,)),
            dma((32,)), dma((32,)),
            dma((16,)), dma((16,)),
            dma((2,)), dma((2,)),
        ],
        compiler_params=pltpu.CompilerParams(
            collective_id=0, has_side_effects=True, vmem_limit_bytes=56 << 20
        ),
        cost_estimate=pl.CostEstimate(flops=60_000_000, bytes_accessed=5_000_000, transcendentals=32_768),
        name="wave_step",
    )(tables(), spectra, u_wind, wind_dir, sea_mask)


def solution(mesh):
    return jax.shard_map(
        shards,
        mesh=mesh,
        in_specs=(P("comp", None, None, "grid"), P(None, "grid"), P(None, "grid"), P(None, "grid")),
        out_specs=P("comp", None, None, "grid"),
        check_vma=False,
    )
```

time: 297 us -> 159 us (0.54)
  the two profiles are of different devices: /device:TPU:23 before, /device:TPU:448 now
where the time goes in v1:
time: 159 us; the launch traced here: 156 us
  Pallas kernels  147 us (92%)
  local copies, waits for them, and re-layouts  9.06 us (6%)
    pallas_call x1, Pallas kernels, shards(): pl.pallas_call(kernel, out_shape=jax.ShapeDtypeStruct(spectra.shape, f32)...  147 us
    unnamed x1, local copies, waits for them, and re-layouts  4.55 us
    pallas_call x1, local copies, waits for them, and re-layouts, shards(): pl.pallas_call(kernel, out_shape=jax.ShapeDtypeStruct(spectra.shape, f32)...  4.51 us

profile of v1, /device:TPU:448, one launch (start us, length us, event | category | flops | bytes accessed | tf_op | source)
XLA Modules:
  0.0 156.0 jit_solution(12336978509584971336)
XLA Ops:
  0.0 4.5 %copy.6.x_hbm = f32[1,32,36,512]{3,2,1,0:T(8,128)} copy(f32[1,32,36,512]{3,1,2,0:T(8,128)} %param.5) | data formatting | bytes 4718592 | tf_op args[0]
  4.6 146.9 %wave_step.1 = f32[1,32,36,512]{3,2,1,0:T(8,128)} custom-call(f32[8,128]{1,0:T(8,128)} %constant.2.clone.tab, f32[1,32,36,512]{3,2,1,0:T(8,128)} %copy.6.x_hbm, f32[32,512]{1,0:T(8,128)} %uw.1, f32[32,512]{1,0:T(8,128)} %wd.1, s32[32,512]{1,0:T(8,128)} %mk.1), custom_call_target="tpu_custom_call" | custom-call | flops 60000000 | bytes 5000000 | tf_op jit(solution)/shard_map/wave_step/pallas_call | solution.py:460
  151.5 4.5 %copy.7 = f32[1,32,36,512]{3,1,2,0:T(8,128)} copy(f32[1,32,36,512]{3,2,1,0:T(8,128)} %wave_step.1) | data formatting | bytes 4718592 | tf_op jit(solution)/shard_map/wave_step/pallas_call | solution.py:460

commit v2 on v1

--- a/solution.py
+++ b/solution.py
@@ -51,19 +51,13 @@
     t[2, :NK] = WIND * w
     t[3, :NK] = w / GRAVITY
     t[4, :NK] = GRAVITY / (2.0 * w) * ADVECT_STEP / (EARTH_RADIUS * CELL_RADIANS)
-    i = np.arange(LAT)
-    cell = np.cos(np.radians(BAND_CENTRE + (i - (LAT - 1) / 2.0) * CELL_DEGREES))
-    upper = np.cos(np.radians(BAND_CENTRE + (i + 1 - LAT / 2.0) * CELL_DEGREES))
-    lower = np.cos(np.radians(BAND_CENTRE + (i - LAT / 2.0) * CELL_DEGREES))
-    t[5, :LAT] = upper / cell
-    t[6, :LAT] = lower / cell
     return t.astype(np.float32)
 
 
 def kernel(
     tab, x_hbm, uw, wd, mk, o_hbm,
     xbuf, obuf, sbuf, ebuf, tbuf, above, below, incr, ibuf, post,
-    eux, edx, d1x, d2x, bus, bds, cen, swept, ybuf, taps, rowinv,
+    eux, edx, d1x, d2x, bus, bds, cen, rowinv, facehi, facelo,
     pack_l, pack_r, halo_l, halo_r,
     load_s, store_s, zin_s, zin_r, hal_s, hal_r, bak_s, bak_r, zout_s, zout_r, lon_s, lon_r,
 ):
@@ -153,15 +147,21 @@
         load(i).wait()
         for dz in (2, 1, 3, 0):
             rg = zpeer(dz)
-            piece = jnp.swapaxes(xbuf[i, rows8(rg)], 0, 1)
-            piece = piece * mk[rows8(rg), lanes(i)].astype(f32)[None]
-            sbuf[i, rg] = piece
-            if dz == 0:
-                ebuf[i, 4 + z] = piece
-            else:
-                if i == 0 and dz == 2:
-                    pl.semaphore_wait(barrier, 7)
+            sea = mk[rows8(rg), lanes(i)].astype(f32)
+
+            @pl.loop(0, NTH // JB)
+            def _(b):
+                at = pl.ds(b * JB, JB)
+                piece = xbuf[i, at, rows8(rg)] * sea[None]
+                sbuf[i, rg, at] = piece
+                if dz == 0:
+                    ebuf[i, 4 + z, at] = piece
+
+            if i == 0 and dz == 2:
+                pl.semaphore_wait(barrier, 7)
+            if i == 0 and dz:
                 zin(i, dz).start()
+        send_halo(i, z)
 
     wind_w = tab[2, me]
     inv_cel = tab[3, me]
@@ -180,31 +180,30 @@
 
     def constants():
         row = lax.broadcasted_iota(jnp.int32, (LAT, LANES), 0).astype(f32)
-        lat = BAND_CENTRE + (row - (LAT - 1) / 2.0) * CELL_DEGREES
-        rowinv[...] = 1.0 / jnp.cos(lat * (math.pi / 180.0))
-        j = lax.broadcasted_iota(jnp.int32, (NTH, LANES), 0).astype(f32)
-        c = courant * jnp.sin(j * (2.0 * math.pi / NTH))
-        q = (1.0 - c * c) / 6.0
-        pos = c >= 0.0
-        taps[0] = c * jnp.where(pos, -q, 0.0)
-        taps[1] = c * (0.5 + 0.5 * c + jnp.where(pos, 2.0 * q, -q))
-        taps[2] = c * (0.5 - 0.5 * c + jnp.where(pos, -q, 2.0 * q))
-        taps[3] = c * jnp.where(pos, 0.0, -q)
+
+        def cosine(offset):
+            return jnp.cos((BAND_CENTRE + (row - offset) * CELL_DEGREES) * (math.pi / 180.0))
+
+        inverse = 1.0 / cosine((LAT - 1) / 2.0)
+        rowinv[...] = inverse
+        facehi[...] = cosine(LAT / 2.0 - 1.0) * inverse
+        facelo[...] = cosine(LAT / 2.0) * inverse
         for i in range(4):
             below[i, 3] = jnp.zeros((NTH, 8, LANES), f32)
-        ybuf[0:2] = jnp.zeros((2, NTH, LANES), f32)
-        ybuf[LAT + 2 : LAT + 4] = jnp.zeros((2, NTH, LANES), f32)
+
+    def send_halo(i, f):
+        hal_up(i, f).start()
+
+        @pl.when(f < 3)
+        def _():
+            hal_dn(i, f).start()
 
     def forward(i):
-        for dz in range(4):
-            f = zfrom(dz)
-            if dz:
-                zin(i, dz).wait_recv()
-            hal_up(i, f).start()
-
-            @pl.when(f < 3)
-            def _():
-                hal_dn(i, f).start()
+        for dz in (1, 2, 3):
+            zin(i, dz).wait_recv()
+            if i < 3:
+                zin(i + 1, dz).start()
+            send_halo(i, zfrom(dz))
 
     def interact(i):
         for f in range(4):
@@ -331,90 +330,98 @@
         lon_to_right().start()
         lon_to_left().start()
 
-    def sweep_x(chunks, rg, j, positive, edge_l, edge_r):
-        c = (courant * tab[0, j]) * rowinv[rg * 8 : rg * 8 + 8]
+    sub = lax.broadcasted_iota(jnp.int32, (8, LANES), 0)
+
+    def shift(here, other, by, axis):
+        size = LANES if axis else 8
+        place = lane if axis else sub
+        if by > 0:
+            return pltpu.roll(jnp.where(place >= size - by, other, here), by, axis)
+        return pltpu.roll(jnp.where(place < -by, other, here), size + by, axis)
+
+    def sweep_x(c, v, left, right, positive):
+        c = c if positive else -c
         q = (1.0 - c * c) * (1.0 / 6.0)
-        one = -q
+        mid = 0.5 + 0.5 * c + 2.0 * q
+        far = 0.5 - 0.5 * c - q
+        k_next, k_here = c * far, 1.0 - c * (mid - far)
+        k_back, k_back2 = c * (q + mid), c * q
+        outs = []
+        for here, low, high in zip(v, left, right, strict=True):
+            up, dn = (low, high) if positive else (high, low)
+            way = 1 if positive else -1
+            nxt = shift(here, dn, -way, 1)
+            back = shift(here, up, way, 1)
+            back2 = shift(here, up, 2 * way, 1)
+            outs.append(k_here * here - k_next * nxt + k_back * back - k_back2 * back2)
+        return outs
+
+    def sweep_y(c, u, positive):
+        q = (1.0 - c * c) * (1.0 / 6.0)
+        zero = jnp.zeros((8, LANES), f32)
+        tiles = [zero, *u, zero]
+        faces = []
         if positive:
-            mid = 0.5 + 0.5 * c + 2.0 * q
-            far = 0.5 - 0.5 * c - q
+            t_back, t_here, t_next = -q * c, c * (0.5 + 0.5 * c + 2.0 * q), c * (0.5 - 0.5 * c - q)
         else:
-            mid = 0.5 - 0.5 * c + 2.0 * q
-            far = 0.5 + 0.5 * c - q
-        sign = c if positive else -c
-        k_next, k_here = sign * far, sign * (mid - far)
-        k_back, k_back2 = sign * (one - mid), sign * one
-        k_here = 1.0 - k_here
+            t_here, t_next, t_next2 = c * (0.5 + 0.5 * c - q), c * (0.5 - 0.5 * c + 2.0 * q), -q * c
+        for r in range(5):
+            here = tiles[r]
+            high = tiles[r + 1]
+            face = t_here * here + t_next * shift(here, high, -1, 0)
+            if positive:
+                if r:
+                    face = face + t_back * shift(here, tiles[r - 1], 1, 0)
+            else:
+                face = face + t_next2 * shift(here, high, -2, 0)
+            faces.append(face)
+        outs = []
+        for r in range(4):
+            over, under = faces[r + 1], shift(faces[r + 1], faces[r], 1, 0)
+            at = slice(r * 8, r * 8 + 8)
+            outs.append(u[r] - (facehi[at] * over - facelo[at] * under))
+        return outs
+
+    def propagate(chunks):
+        @pl.loop(0, NTH // 4)
+        def _(t):
+            for quarter in range(4):
+                j = t + 9 * quarter
+                x_pos, y_pos = quarter in (0, 3), quarter in (0, 1)
+                swept = [[None] * 4 for _ in chunks]
+                for rg in range(4):
+                    v = {col: post[ORDER.index(col), rg, j] for col in range(4)}
+                    if 0 in chunks:
+                        v[-1] = has_left * pltpu.roll(halo_l[rg], 126 - 2 * j, 1)
+                    if 3 in chunks:
+                        v[4] = has_right * pltpu.roll(halo_r[rg], LANES - 2 * j, 1)
+                    outs = sweep_x(
+                        (courant * tab[0, j]) * rowinv[rg * 8 : rg * 8 + 8],
+                        [v[col] for col in chunks],
+                        [v[col - 1] for col in chunks],
+                        [v[col + 1] for col in chunks],
+                        x_pos,
+                    )
+                    for n, out in enumerate(outs):
+                        sea = mk[rg * 8 : rg * 8 + 8, lanes(ORDER.index(chunks[n]))]
+                        swept[n][rg] = out * sea.astype(f32)
+                for n, col in enumerate(chunks):
+                    outs = sweep_y(courant * tab[1, j], swept[n], y_pos)
+                    for rg in range(4):
+                        at = slice(rg * 8, rg * 8 + 8)
+                        sea = mk[at, lanes(ORDER.index(col))].astype(f32)
+                        obuf[ORDER.index(col), j, at] = outs[rg] * sea
+
         for col in chunks:
-            v = post[ORDER.index(col), rg, j]
-            if col == 0:
-                vl = edge_l
-            else:
-                vl = post[ORDER.index(col - 1), rg, j]
-            if col == 3:
-                vr = edge_r
-            else:
-                vr = post[ORDER.index(col + 1), rg, j]
-            if positive:
-                nxt = pltpu.roll(jnp.where(lane == 0, vr, v), LANES - 1, 1)
-                back = pltpu.roll(jnp.where(lane == LANES - 1, vl, v), 1, 1)
-                back2 = pltpu.roll(jnp.where(lane >= LANES - 2, vl, v), 2, 1)
-            else:
-                nxt = pltpu.roll(jnp.where(lane == LANES - 1, vl, v), 1, 1)
-                back = pltpu.roll(jnp.where(lane == 0, vr, v), LANES - 1, 1)
-                back2 = pltpu.roll(jnp.where(lane < 2, vr, v), LANES - 2, 1)
-            out = k_here * v - (k_next * nxt + k_back * back - k_back2 * back2)
-            swept[ORDER.index(col), rg, j] = out
-
-    def propagate(chunks):
-        for rg in range(4):
-
-            @pl.loop(0, NTH // 2)
-            def _(t):
-                for positive in (True, False):
-                    j = lax.rem(t + 27, NTH) if positive else t + 9
-                    edge_l = edge_r = None
-                    if 0 in chunks:
-                        edge_l = has_left * pltpu.roll(halo_l[rg], 126 - 2 * j, 1)
-                    if 3 in chunks:
-                        edge_r = has_right * pltpu.roll(halo_r[rg], LANES - 2 * j, 1)
-                    sweep_x(chunks, rg, j, positive, edge_l, edge_r)
-
-        for col in chunks:
-            i = ORDER.index(col)
-            for rg in range(4):
-                sea = mk[rg * 8 : rg * 8 + 8, lanes(i)].astype(f32)
-                ybuf[2 + rg * 8 : 10 + rg * 8] = jnp.swapaxes(swept[i, rg] * sea[None], 0, 1)
-
-            def flux(r):
-                return (
-                    taps[0] * ybuf[r + 1] + taps[1] * ybuf[r + 2]
-                    + taps[2] * ybuf[r + 3] + taps[3] * ybuf[r + 4]
-                )
-
-            def rows(block, under):
-                sea = mk[rows8(block), lanes(i)].astype(f32)
-                for s in range(8):
-                    r = block * 8 + s
-                    over = flux(r)
-                    out = ybuf[r + 2] - (tab[5, r] * over - tab[6, r] * under)
-                    obuf[i, r] = out * sea[s : s + 1]
-                    under = over
-                return under
-
-            first = taps[2] * ybuf[2] + taps[3] * ybuf[3]
-            lax.fori_loop(0, LAT // 8, rows, first)
-            store(i).start()
-
-    prepare(0)
-    prepare(1)
+            store(ORDER.index(col)).start()
+
+    for i in range(4):
+        prepare(i)
     constants()
     grow(0)
     forward(0)
-    prepare(2)
     grow(1)
     forward(1)
-    prepare(3)
     interact(0)
     grow(2)
     forward(2)
@@ -457,9 +464,10 @@
     tile = (NTH, 8, LANES)
     vmem, dma = pltpu.VMEM, pltpu.SemaphoreType.DMA
     inner = pl.BlockSpec(memory_space=pltpu.VMEM)
-    return pl.pallas_call(
+    columns = jnp.transpose(spectra, (0, 2, 1, 3))
+    result = pl.pallas_call(
         kernel,
-        out_shape=jax.ShapeDtypeStruct(spectra.shape, f32),
+        out_shape=jax.ShapeDtypeStruct(columns.shape, f32),
         in_specs=[
             pl.BlockSpec(memory_space=pltpu.SMEM),
             pl.BlockSpec(memory_space=pl.ANY),
@@ -467,8 +475,8 @@
         ],
         out_specs=pl.BlockSpec(memory_space=pl.ANY),
         scratch_shapes=[
-            vmem((4, LAT, NTH, LANES), f32),
-            vmem((4, LAT, NTH, LANES), f32),
+            vmem((4, NTH, LAT, LANES), f32),
+            vmem((4, NTH, LAT, LANES), f32),
             vmem((4, 4) + tile, f32),
             vmem((4, 11) + tile, f32),
             vmem((4, 11) + tile, f32),
@@ -484,9 +492,8 @@
             vmem((4,) + tile, f32),
             vmem((4,) + tile, f32),
             vmem((4,) + tile, f32),
-            vmem((4, 4) + tile, f32),
-            vmem((LAT + 4, NTH, LANES), f32),
-            vmem((4, NTH, LANES), f32),
+            vmem((LAT, LANES), f32),
+            vmem((LAT, LANES), f32),
             vmem((LAT, LANES), f32),
             vmem((4, 8, LANES), f32),
             vmem((4, 8, LANES), f32),
@@ -504,7 +511,8 @@
         ),
         cost_estimate=pl.CostEstimate(flops=60_000_000, bytes_accessed=5_000_000, transcendentals=32_768),
         name="wave_step",
-    )(tables(), spectra, u_wind, wind_dir, sea_mask)
+    )(tables(), columns, u_wind, wind_dir, sea_mask)
+    return jnp.transpose(result, (0, 2, 1, 3))
 
 
 def solution(mesh):

time: 159 us -> 128 us (0.81)
  the two profiles are of different devices: /device:TPU:448 before, /device:TPU:95 now
where the time goes in v2:
time: 128 us
  Pallas kernels  124 us (97%)
  local copies, waits for them, and re-layouts  3.41 us (3%)
    pallas_call x1, Pallas kernels, shards(): pl.pallas_call(kernel, out_shape=jax.ShapeDtypeStruct(columns.shape, f32)...  124 us
    unnamed x1, local copies, waits for them, and re-layouts  3.41 us

profile of v2, /device:TPU:95, one launch (start us, length us, event | category | flops | bytes accessed | tf_op | source)
XLA Modules:
  0.0 127.6 jit_solution(1972511297740437961)
XLA Ops:
  0.0 124.2 %wave_step.1 = f32[1,36,32,512]{3,2,1,0:T(8,128)} custom-call(f32[8,128]{1,0:T(8,128)} %constant.2.clone.tab, f32[1,36,32,512]{3,2,1,0:T(8,128)} %bitcast.3, f32[32,512]{1,0:T(8,128)} %uw.1, f32[32,512]{1,0:T(8,128)} %wd.1, s32[32,512]{1,0:T(8,128)} %mk.1), custom_call_target="tpu_custom_call" | custom-call | flops 60000000 | bytes 5000000 | tf_op jit(solution)/shard_map/wave_step/pallas_call | solution.py:468
  124.2 3.4 %copy.7 = f32[1,32,36,512]{3,1,2,0:T(8,128)} copy(f32[1,32,36,512]{3,1,2,0:T(8,128)} %bitcast.2) | data formatting | bytes 4718592

commit v3 on v2

--- a/solution.py
+++ b/solution.py
@@ -37,6 +37,7 @@
 
 ORDER = (0, 3, 1, 2)
 LANES = 128
+HALF = NTH // 2
 JB = 4
 PAD = 4
 
@@ -84,10 +85,14 @@
             x_hbm.at[0, :, :, pl.ds(ORDER[i] * LANES, LANES)], xbuf.at[i], load_s.at[i]
         )
 
-    def store(i):
+    def store(i, half):
+        at = pl.ds(half * HALF, HALF)
         return pltpu.make_async_copy(
-            obuf.at[i], o_hbm.at[0, :, :, pl.ds(ORDER[i] * LANES, LANES)], store_s.at[i]
+            obuf.at[i, at], o_hbm.at[0, at, :, pl.ds(ORDER[i] * LANES, LANES)], store_s.at[i * 2 + half]
         )
+
+    def part(i, half):
+        return pl.ds(half * HALF, HALF) if i == 3 else pl.ds(0, NTH)
 
     def remote(src, dst, ss, rs, **to):
         return pltpu.make_async_remote_copy(
@@ -107,18 +112,18 @@
         k = i * 8 + 4 + f
         return remote(ebuf.at[i, 4 + f], ebuf.at[i, 8 + f], hal_s.at[k], hal_r.at[k], comp=y_dn)
 
-    def bak_dn(i, m):
-        k = i * 8 + m
-        return remote(tbuf.at[i, m], above.at[i, m], bak_s.at[k], bak_r.at[k], comp=y_dn)
-
-    def bak_up(i, m):
-        k = i * 8 + 4 + m
-        return remote(tbuf.at[i, 8 + m], below.at[i, m], bak_s.at[k], bak_r.at[k], comp=y_up)
-
-    def zout(i, dz):
-        p = zpeer(dz)
-        k = i * 4 + dz
-        return remote(incr.at[i, p], ibuf.at[i, z], zout_s.at[k], zout_r.at[k], comp=y * 4 + p)
+    def bak_dn(i, m, half=0):
+        k, at = (i + half) * 8 + m, part(i, half)
+        return remote(tbuf.at[i, m, at], above.at[i, m, at], bak_s.at[k], bak_r.at[k], comp=y_dn)
+
+    def bak_up(i, m, half=0):
+        k, at = (i + half) * 8 + 4 + m, part(i, half)
+        return remote(tbuf.at[i, 8 + m, at], below.at[i, m, at], bak_s.at[k], bak_r.at[k], comp=y_up)
+
+    def zout(i, dz, half=0):
+        p, at = zpeer(dz), part(i, half)
+        k = (i + half) * 4 + dz
+        return remote(incr.at[i, p, at], ibuf.at[i, z, at], zout_s.at[k], zout_r.at[k], comp=y * 4 + p)
 
     def lon_to_right():
         return remote(pack_r, halo_l, lon_s.at[0], lon_r.at[0], grid=g_right)
@@ -279,34 +284,44 @@
             tbuf[i, 9, j] = U1 * bu[2] + U0 * bu[3]
             tbuf[i, 10, j] = U1 * bu[3]
 
-        for m in range(4):
-            bak_dn(i, m).start()
-            if m < 3:
-                bak_up(i, m).start()
-
-    def gather(i):
         for dz in (1, 2, 3, 0):
             m = zpeer(dz)
-            bak_dn(i, m).wait_recv()
+            bak_dn(i, m).start()
 
             @pl.when(m < 3)
             def _():
-                bak_up(i, m).wait_recv()
-
-            total = tbuf[i, 4 + m] + has_hi * above[i, m] + has_lo * below[i, m]
+                bak_up(i, m).start()
+
+    def gather(i, half=0):
+        at = part(i, half)
+        for dz in (1, 2, 3, 0):
+            m = zpeer(dz)
+            more = i == 3 and half == 0
+            bak_dn(i, m, half).wait_recv()
+            if more:
+                bak_dn(i, m, 1).start()
+
+            @pl.when(m < 3)
+            def _():
+                bak_up(i, m, half).wait_recv()
+                if more:
+                    bak_up(i, m, 1).start()
+
+            total = tbuf[i, 4 + m, at] + has_hi * above[i, m, at] + has_lo * below[i, m, at]
             if dz == 0:
-                ibuf[i, z] = total
+                ibuf[i, z, at] = total
             else:
-                incr[i, m] = total
-                zout(i, dz).start()
-
-    def finish(i):
+                incr[i, m, at] = total
+                zout(i, dz, half).start()
+
+    def finish(i, half=0):
         for dz in (1, 2, 3):
-            zout(i, dz).wait_recv()
-
-        @pl.loop(0, NTH // JB)
+            zout(i, dz, half).wait_recv()
+        whole = part(i, half).size
+
+        @pl.loop(0, whole // 6)
         def _(b):
-            at = pl.ds(b * JB, JB)
+            at = pl.ds(half * HALF + b * 6, 6)
             for rg in range(4):
                 post[i, rg, at] = post[i, rg, at] + ibuf[i, rg, at]
 
@@ -314,19 +329,17 @@
 
     def edges():
         first, last = ORDER.index(0), ORDER.index(3)
-        for rg in range(4):
-
-            def step(j, acc):
-                a, b = acc
-                here = (lane == 2 * j) | (lane == 2 * j + 1)
+
+        @pl.loop(0, 4)
+        def _(rg):
+            a, b = post[first, rg, 0], pltpu.roll(post[last, rg, 0], 2, 1)
+            for j in range(1, NTH):
+                here = lane >= 2 * j
                 a = jnp.where(here, pltpu.roll(post[first, rg, j], 2 * j, 1), a)
                 b = jnp.where(here, pltpu.roll(post[last, rg, j], 2 * j + 2, 1), b)
-                return a, b
-
-            zero = jnp.zeros((8, LANES), f32)
-            a, b = lax.fori_loop(0, NTH, step, (zero, zero), unroll=4)
             pack_l[rg] = a
             pack_r[rg] = b
+
         lon_to_right().start()
         lon_to_left().start()
 
@@ -382,10 +395,10 @@
             outs.append(u[r] - (facehi[at] * over - facelo[at] * under))
         return outs
 
-    def propagate(chunks):
+    def propagate(chunks, half):
         @pl.loop(0, NTH // 4)
         def _(t):
-            for quarter in range(4):
+            for quarter in (2 * half, 2 * half + 1):
                 j = t + 9 * quarter
                 x_pos, y_pos = quarter in (0, 3), quarter in (0, 1)
                 swept = [[None] * 4 for _ in chunks]
@@ -413,7 +426,7 @@
                         obuf[ORDER.index(col), j, at] = outs[rg] * sea
 
         for col in chunks:
-            store(ORDER.index(col)).start()
+            store(ORDER.index(col), half).start()
 
     for i in range(4):
         prepare(i)
@@ -436,25 +449,34 @@
     gather(2)
     finish(1)
     edges()
-    gather(3)
+    gather(3, 0)
+    gather(3, 1)
     finish(2)
     lon_to_right().wait_recv()
     lon_to_left().wait_recv()
-    propagate((0,))
-    finish(3)
-    propagate((1, 2, 3))
+    propagate((0,), 0)
+    propagate((0,), 1)
+    finish(3, 0)
+    propagate((1, 2, 3), 0)
+    finish(3, 1)
+    propagate((1, 2, 3), 1)
 
     for i in range(4):
         for dz in (1, 2, 3):
             zin(i, dz).wait_send()
-            zout(i, dz).wait_send()
         for f in range(4):
             hal_up(i, f).wait_send()
-            bak_dn(i, f).wait_send()
         for f in range(3):
             hal_dn(i, f).wait_send()
-            bak_up(i, f).wait_send()
-        store(i).wait()
+        for half in range(2 if i == 3 else 1):
+            for dz in (1, 2, 3):
+                zout(i, dz, half).wait_send()
+            for m in range(4):
+                bak_dn(i, m, half).wait_send()
+            for m in range(3):
+                bak_up(i, m, half).wait_send()
+        store(i, 0).wait()
+        store(i, 1).wait()
     lon_to_right().wait_send()
     lon_to_left().wait_send()
 
@@ -499,11 +521,11 @@
             vmem((4, 8, LANES), f32),
             vmem((4, 8, LANES), f32),
             vmem((4, 8, LANES), f32),
-            dma((4,)), dma((4,)),
+            dma((4,)), dma((8,)),
             dma((16,)), dma((16,)),
             dma((32,)), dma((32,)),
-            dma((32,)), dma((32,)),
-            dma((16,)), dma((16,)),
+            dma((40,)), dma((40,)),
+            dma((20,)), dma((20,)),
             dma((2,)), dma((2,)),
         ],
         compiler_params=pltpu.CompilerParams(

time: 128 us -> 125 us (0.977)
  the two profiles are of different devices: /device:TPU:95 before, /device:TPU:23 now
where the time goes in v3:
time: 125 us
  Pallas kernels  121 us (97%)
  local copies, waits for them, and re-layouts  3.41 us (3%)
    pallas_call x1, Pallas kernels, shards(): pl.pallas_call(kernel, out_shape=jax.ShapeDtypeStruct(columns.shape, f32)...  121 us
    unnamed x1, local copies, waits for them, and re-layouts  3.41 us

profile of v3, /device:TPU:23, one launch (start us, length us, event | category | flops | bytes accessed | tf_op | source)
XLA Modules:
  0.0 124.8 jit_solution(18176611556064629499)
XLA Ops:
  0.0 121.4 %wave_step.1 = f32[1,36,32,512]{3,2,1,0:T(8,128)} custom-call(f32[8,128]{1,0:T(8,128)} %constant.2.clone.tab, f32[1,36,32,512]{3,2,1,0:T(8,128)} %bitcast.3, f32[32,512]{1,0:T(8,128)} %uw.1, f32[32,512]{1,0:T(8,128)} %wd.1, s32[32,512]{1,0:T(8,128)} %mk.1), custom_call_target="tpu_custom_call" | custom-call | flops 60000000 | bytes 5000000 | tf_op jit(solution)/shard_map/wave_step/pallas_call | solution.py:490
  121.4 3.4 %copy.7 = f32[1,32,36,512]{3,1,2,0:T(8,128)} copy(f32[1,32,36,512]{3,1,2,0:T(8,128)} %bitcast.2) | data formatting | bytes 4718592

commit v4 on v3

--- a/solution.py
+++ b/solution.py
@@ -36,6 +36,7 @@
 W_CROSS = 0.2 / (1.0 - LAMBDA * LAMBDA) ** 4
 
 ORDER = (0, 3, 1, 2)
+WINDOW = (0, 1, 0, 1)
 LANES = 128
 HALF = NTH // 2
 JB = 4
@@ -53,6 +54,22 @@
     t[3, :NK] = w / GRAVITY
     t[4, :NK] = GRAVITY / (2.0 * w) * ADVECT_STEP / (EARTH_RADIUS * CELL_RADIANS)
     return t.astype(np.float32)
+
+
+def halo_ups(i):
+    return range(1, 4) if WINDOW[i] else range(4)
+
+
+def halo_dns(i):
+    return range(4) if WINDOW[i] else range(3)
+
+
+def back_ups(i):
+    return range(4) if WINDOW[i] else range(3)
+
+
+def back_dns(i):
+    return range(1, 4) if WINDOW[i] else range(4)
 
 
 def kernel(
@@ -91,6 +108,23 @@
             obuf.at[i, at], o_hbm.at[0, at, :, pl.ds(ORDER[i] * LANES, LANES)], store_s.at[i * 2 + half]
         )
 
+    def travels(i, f, four, action):
+        if four:
+            action()
+        else:
+
+            @pl.when(f >= 1 if WINDOW[i] else f < 3)
+            def _():
+                action()
+
+    def halo_each(i, f, up, down):
+        travels(i, f, WINDOW[i] == 0, up)
+        travels(i, f, WINDOW[i] == 1, down)
+
+    def back_each(i, m, up, down):
+        travels(i, m, WINDOW[i] == 1, up)
+        travels(i, m, WINDOW[i] == 0, down)
+
     def part(i, half):
         return pl.ds(half * HALF, HALF) if i == 3 else pl.ds(0, NTH)
 
@@ -194,14 +228,13 @@
         facehi[...] = cosine(LAT / 2.0 - 1.0) * inverse
         facelo[...] = cosine(LAT / 2.0) * inverse
         for i in range(4):
-            below[i, 3] = jnp.zeros((NTH, 8, LANES), f32)
+            if WINDOW[i]:
+                above[i, 0] = jnp.zeros((NTH, 8, LANES), f32)
+            else:
+                below[i, 3] = jnp.zeros((NTH, 8, LANES), f32)
 
     def send_halo(i, f):
-        hal_up(i, f).start()
-
-        @pl.when(f < 3)
-        def _():
-            hal_dn(i, f).start()
+        halo_each(i, f, lambda: hal_up(i, f).start(), lambda: hal_dn(i, f).start())
 
     def forward(i):
         for dz in (1, 2, 3):
@@ -211,24 +244,27 @@
             send_halo(i, zfrom(dz))
 
     def interact(i):
-        for f in range(4):
+        for f in halo_ups(i):
             hal_up(i, f).wait_recv()
-        for f in range(3):
+        for f in halo_dns(i):
             hal_dn(i, f).wait_recv()
+        w = WINDOW[i]
 
         @pl.loop(0, 4)
         def _(k):
-            lo_a = jnp.where(k < 4, has_lo, 1.0) * D1W
-            lo_b = jnp.where(k < 3, has_lo, 1.0) * D0W
-            hi_a = jnp.where(k >= 2, has_hi, 1.0) * U0
-            hi_b = jnp.where(k >= 1, has_hi, 1.0) * U1
+            beyond = k >= 4 - w
+            low = jnp.where(beyond, has_hi, 1.0)
+            lo_a = jnp.where(k < 4 - w, has_lo, low) * D1W
+            lo_b = jnp.where(k < 3 - w, has_lo, low) * D0W
+            hi_a = jnp.where((k >= 2 - w) & ~beyond, has_hi, 1.0) * U0
+            hi_b = jnp.where((k >= 1 - w) & ~beyond, has_hi, 1.0) * U1
 
             @pl.loop(0, NTH // JB)
             def _(b):
                 at = pl.ds(b * JB, JB)
                 to = pl.ds(b * JB + PAD, JB)
-                eux[to] = hi_a * ebuf[i, k + 6, at] + hi_b * ebuf[i, k + 7, at]
-                edx[to] = lo_b * ebuf[i, k + 1, at] + lo_a * ebuf[i, k, at]
+                eux[to] = hi_a * ebuf[i, k + w + 6, at] + hi_b * ebuf[i, k + w + 7, at]
+                edx[to] = lo_b * ebuf[i, k + w + 1, at] + lo_a * ebuf[i, k + w, at]
 
             for ref in (eux, edx):
                 ref[0:PAD] = ref[NTH : NTH + PAD]
@@ -242,7 +278,7 @@
                 def ed(o):
                     return edx[pl.ds(b * JB + PAD + o, JB)]
 
-                e = ebuf[i, k + 4, pl.ds(b * JB, JB)]
+                e = ebuf[i, k + w + 4, pl.ds(b * JB, JB)]
 
                 def delta(plus, minus):
                     return e * (e * (W_UP * plus + W_DOWN * minus) - W_CROSS * plus * minus)
@@ -272,42 +308,56 @@
         def _(j):
             bd = [bds[k, j] for k in range(4)]
             bu = [bus[k, j] for k in range(4)]
-            tbuf[i, 0, j] = D1W * bd[0]
-            tbuf[i, 1, j] = D0W * bd[0] + D1W * bd[1]
-            tbuf[i, 2, j] = D0W * bd[1] + D1W * bd[2]
-            tbuf[i, 3, j] = D0W * bd[2] + D1W * bd[3]
-            tbuf[i, 4, j] = cen[0, j] + D0W * bd[3]
-            tbuf[i, 5, j] = cen[1, j]
-            tbuf[i, 6, j] = cen[2, j] + U0 * bu[0]
-            tbuf[i, 7, j] = cen[3, j] + U1 * bu[0] + U0 * bu[1]
-            tbuf[i, 8, j] = U1 * bu[1] + U0 * bu[2]
-            tbuf[i, 9, j] = U1 * bu[2] + U0 * bu[3]
-            tbuf[i, 10, j] = U1 * bu[3]
+            ce = [cen[k, j] for k in range(4)]
+            if w:
+                own = has_hi * bd[3]
+                tbuf[i, 1, j] = D1W * bd[0]
+                tbuf[i, 2, j] = D0W * bd[0] + D1W * bd[1]
+                tbuf[i, 3, j] = D0W * bd[1] + D1W * bd[2]
+                tbuf[i, 4, j] = D0W * bd[2] + D1W * own
+                tbuf[i, 5, j] = ce[0] + D0W * own
+                tbuf[i, 6, j] = ce[1]
+                tbuf[i, 7, j] = ce[2] + U0 * bu[0]
+                tbuf[i, 8, j] = ce[3] + has_hi * (U1 * bu[0] + U0 * bu[1])
+                tbuf[i, 9, j] = has_hi * (U1 * bu[1] + U0 * bu[2])
+                tbuf[i, 10, j] = has_hi * (U1 * bu[2]) + U0 * bu[3]
+                tbuf[i, 11, j] = U1 * bu[3]
+            else:
+                tbuf[i, 0, j] = D1W * bd[0]
+                tbuf[i, 1, j] = D0W * bd[0] + D1W * bd[1]
+                tbuf[i, 2, j] = D0W * bd[1] + D1W * bd[2]
+                tbuf[i, 3, j] = D0W * bd[2] + D1W * bd[3]
+                tbuf[i, 4, j] = ce[0] + D0W * bd[3]
+                tbuf[i, 5, j] = ce[1]
+                tbuf[i, 6, j] = ce[2] + U0 * bu[0]
+                tbuf[i, 7, j] = ce[3] + U1 * bu[0] + U0 * bu[1]
+                tbuf[i, 8, j] = U1 * bu[1] + U0 * bu[2]
+                tbuf[i, 9, j] = U1 * bu[2] + U0 * bu[3]
+                tbuf[i, 10, j] = U1 * bu[3]
 
         for dz in (1, 2, 3, 0):
             m = zpeer(dz)
-            bak_dn(i, m).start()
-
-            @pl.when(m < 3)
-            def _():
-                bak_up(i, m).start()
+            back_each(i, m, lambda: bak_up(i, m).start(), lambda: bak_dn(i, m).start())
 
     def gather(i, half=0):
         at = part(i, half)
         for dz in (1, 2, 3, 0):
             m = zpeer(dz)
             more = i == 3 and half == 0
-            bak_dn(i, m, half).wait_recv()
-            if more:
-                bak_dn(i, m, 1).start()
-
-            @pl.when(m < 3)
-            def _():
+
+            def up():
                 bak_up(i, m, half).wait_recv()
                 if more:
                     bak_up(i, m, 1).start()
 
-            total = tbuf[i, 4 + m, at] + has_hi * above[i, m, at] + has_lo * below[i, m, at]
+            def down():
+                bak_dn(i, m, half).wait_recv()
+                if more:
+                    bak_dn(i, m, 1).start()
+
+            back_each(i, m, up, down)
+            under = 1.0 if WINDOW[i] else has_lo
+            total = tbuf[i, 4 + m, at] + has_hi * above[i, m, at] + under * below[i, m, at]
             if dz == 0:
                 ibuf[i, z, at] = total
             else:
@@ -464,17 +514,17 @@
     for i in range(4):
         for dz in (1, 2, 3):
             zin(i, dz).wait_send()
-        for f in range(4):
+        for f in halo_ups(i):
             hal_up(i, f).wait_send()
-        for f in range(3):
+        for f in halo_dns(i):
             hal_dn(i, f).wait_send()
         for half in range(2 if i == 3 else 1):
             for dz in (1, 2, 3):
                 zout(i, dz, half).wait_send()
-            for m in range(4):
+            for m in back_ups(i):
+                bak_up(i, m, half).wait_send()
+            for m in back_dns(i):
                 bak_dn(i, m, half).wait_send()
-            for m in range(3):
-                bak_up(i, m, half).wait_send()
         store(i, 0).wait()
         store(i, 1).wait()
     lon_to_right().wait_send()
@@ -492,7 +542,7 @@
         out_shape=jax.ShapeDtypeStruct(columns.shape, f32),
         in_specs=[
             pl.BlockSpec(memory_space=pltpu.SMEM),
-            pl.BlockSpec(memory_space=pl.ANY),
+            pl.BlockSpec(memory_space=pltpu.HBM),
             inner, inner, inner,
         ],
         out_specs=pl.BlockSpec(memory_space=pl.ANY),
@@ -500,8 +550,8 @@
             vmem((4, NTH, LAT, LANES), f32),
             vmem((4, NTH, LAT, LANES), f32),
             vmem((4, 4) + tile, f32),
-            vmem((4, 11) + tile, f32),
-            vmem((4, 11) + tile, f32),
+            vmem((4, 12) + tile, f32),
+            vmem((4, 12) + tile, f32),
             vmem((4, 4) + tile, f32),
             vmem((4, 4) + tile, f32),
             vmem((4, 4) + tile, f32),
@@ -529,7 +579,7 @@
             dma((2,)), dma((2,)),
         ],
         compiler_params=pltpu.CompilerParams(
-            collective_id=0, has_side_effects=True, vmem_limit_bytes=56 << 20
+            collective_id=0, has_side_effects=True, vmem_limit_bytes=50 << 20
         ),
         cost_estimate=pl.CostEstimate(flops=60_000_000, bytes_accessed=5_000_000, transcendentals=32_768),
         name="wave_step",

time: 125 us -> 124 us (level)
  the two profiles are of different devices: /device:TPU:23 before, /device:TPU:448 now
where the time goes in v4:
time: 124 us; the launch traced here: 123 us
  Pallas kernels  119 us (96%)
  local copies, waits for them, and re-layouts  4.61 us (4%)
    pallas_call x1, Pallas kernels, shards(): pl.pallas_call(kernel, out_shape=jax.ShapeDtypeStruct(columns.shape, f32)...  119 us
    unnamed x9, local copies, waits for them, and re-layouts  4.61 us

profile of v4, /device:TPU:448, one launch (start us, length us, event | category | flops | bytes accessed | tf_op | source)
XLA Modules:
  0.0 123.3 jit_solution(11061934245470989365)
XLA Ops:
  0.0 0.0 copy-start
  0.0 0.8 copy-done
  0.8 0.0 copy-start.1
  0.8 0.8 copy-done.1
  1.7 0.0 copy-start.2
  1.7 0.8 copy-done.2
  2.5 0.0 copy-start.3
  2.5 0.7 copy-done.3
  3.2 118.7 %wave_step.1 = f32[1,36,32,512]{3,2,1,0:T(8,128)S(1)} custom-call(f32[8,128]{1,0:T(8,128)S(1)} %copy-done.3, f32[1,36,32,512]{3,2,1,0:T(8,128)} %bitcast.3, f32[32,512]{1,0:T(8,128)S(1)} %copy-done, f32[32,512]{1,0:T(8,128)S(1)} %copy-done.1, s32[32,512]{1,0:T(8,128)S(1)} %copy-done.2), custom_call_target="tpu_custom_call" | custom-call | flops 60000000 | bytes 5000000 | tf_op jit(solution)/shard_map/wave_step/pallas_call | solution.py:540
  121.9 1.4 %copy.7 = f32[1,32,36,512]{3,1,2,0:T(8,128)} copy(f32[1,32,36,512]{3,1,2,0:T(8,128)S(1)} %bitcast.2) | data formatting | bytes 4718592
Async XLA Ops:
  0.0 0.8 copy-start
  0.8 0.8 copy-start.1
  1.7 0.8 copy-start.2
  2.5 0.7 copy-start.3

commit v5 on v4

--- a/solution.py
+++ b/solution.py
@@ -73,11 +73,11 @@
 
 
 def kernel(
-    tab, x_hbm, uw, wd, mk, o_hbm,
-    xbuf, obuf, sbuf, ebuf, tbuf, above, below, incr, ibuf, post,
+    tab_hbm, x_hbm, uw_hbm, wd_hbm, mk_hbm, o_hbm,
+    tab, uw, wd, mk, xbuf, obuf, sbuf, ebuf, tbuf, above, below, incr, ibuf, post,
     eux, edx, d1x, d2x, bus, bds, cen, rowinv, facehi, facelo,
     pack_l, pack_r, halo_l, halo_r,
-    load_s, store_s, zin_s, zin_r, hal_s, hal_r, bak_s, bak_r, zout_s, zout_r, lon_s, lon_r,
+    load_s, store_s, cell_s, zin_s, zin_r, hal_s, hal_r, bak_s, bak_r, zout_s, zout_r, lon_s, lon_r,
 ):
     f32 = jnp.float32
     me = lax.axis_index("comp")
@@ -165,8 +165,17 @@
     def lon_to_left():
         return remote(pack_l, halo_r, lon_s.at[1], lon_r.at[1], grid=g_left)
 
+    cells = [
+        pltpu.make_async_copy(src, dst, cell_s.at[n])
+        for n, (src, dst) in enumerate(
+            ((mk_hbm, mk), (uw_hbm, uw), (wd_hbm, wd), (tab_hbm, tab))
+        )
+    ]
+    cells[0].start()
     for i in range(4):
         load(i).start()
+    for n in (3, 1, 2):
+        cells[n].start()
 
     barrier = pltpu.get_barrier_semaphore()
     for dz in (1, 2, 3):
@@ -202,9 +211,6 @@
                 zin(i, dz).start()
         send_halo(i, z)
 
-    wind_w = tab[2, me]
-    inv_cel = tab[3, me]
-    courant = tab[4, me]
 
     def grow(i):
         for rg in range(4):
@@ -478,9 +484,13 @@
         for col in chunks:
             store(ORDER.index(col), half).start()
 
+    cells[0].wait()
     for i in range(4):
         prepare(i)
     constants()
+    for n in (1, 2, 3):
+        cells[n].wait()
+    wind_w, inv_cel, courant = tab[2, me], tab[3, me], tab[4, me]
     grow(0)
     forward(0)
     grow(1)
@@ -535,18 +545,22 @@
     f32 = jnp.float32
     tile = (NTH, 8, LANES)
     vmem, dma = pltpu.VMEM, pltpu.SemaphoreType.DMA
-    inner = pl.BlockSpec(memory_space=pltpu.VMEM)
+    outer = pl.BlockSpec(memory_space=pltpu.HBM)
+    shape = u_wind.shape
+    def stay(a):
+        return pltpu.with_memory_space_constraint(a, pltpu.HBM)
+
     columns = jnp.transpose(spectra, (0, 2, 1, 3))
     result = pl.pallas_call(
         kernel,
         out_shape=jax.ShapeDtypeStruct(columns.shape, f32),
         in_specs=[
-            pl.BlockSpec(memory_space=pltpu.SMEM),
-            pl.BlockSpec(memory_space=pltpu.HBM),
-            inner, inner, inner,
+            outer, outer, outer, outer, outer,
         ],
         out_specs=pl.BlockSpec(memory_space=pl.ANY),
         scratch_shapes=[
+            pltpu.SMEM((8, 128), f32),
+            vmem(shape, f32), vmem(shape, f32), vmem(shape, jnp.int32),
             vmem((4, NTH, LAT, LANES), f32),
             vmem((4, NTH, LAT, LANES), f32),
             vmem((4, 4) + tile, f32),
@@ -571,7 +585,7 @@
             vmem((4, 8, LANES), f32),
             vmem((4, 8, LANES), f32),
             vmem((4, 8, LANES), f32),
-            dma((4,)), dma((8,)),
+            dma((4,)), dma((8,)), dma((4,)),
             dma((16,)), dma((16,)),
             dma((32,)), dma((32,)),
             dma((40,)), dma((40,)),
@@ -583,7 +597,7 @@
         ),
         cost_estimate=pl.CostEstimate(flops=60_000_000, bytes_accessed=5_000_000, transcendentals=32_768),
         name="wave_step",
-    )(tables(), columns, u_wind, wind_dir, sea_mask)
+    )(*(stay(a) for a in (jnp.asarray(tables()), columns, u_wind, wind_dir, sea_mask)))
     return jnp.transpose(result, (0, 2, 1, 3))
 
 

time: 124 us -> 120 us (0.968)
  local copies, waits for them, and re-layouts: 4.61 us -> 1.41 us
    unnamed x9 -> x1, local copies, waits for them, and re-layouts: 4.61 us -> 1.41 us
where the time goes in v5:
time: 120 us
  Pallas kernels  118 us (98%)
  local copies, waits for them, and re-layouts  1.41 us (1%)
    pallas_call x1, Pallas kernels, shards(): pl.pallas_call(kernel, out_shape=jax.ShapeDtypeStruct(columns.shape, f32)...  118 us

profile of v5, /device:TPU:448, one launch (start us, length us, event | category | flops | bytes accessed | tf_op | source)
XLA Modules:
  0.0 119.5 jit_solution(4942086541699617330)
XLA Ops:
  0.0 118.1 %wave_step.1 = f32[1,36,32,512]{3,2,1,0:T(8,128)S(1)} custom-call(f32[8,128]{1,0:T(8,128)} %constant.2.clone.tab_hbm, f32[1,36,32,512]{3,2,1,0:T(8,128)} %bitcast.3, f32[32,512]{1,0:T(8,128)} %uw_hbm.1, f32[32,512]{1,0:T(8,128)} %wd_hbm.1, s32[32,512]{1,0:T(8,128)} %mk_hbm.1), custom_call_target="tpu_custom_call" | custom-call | flops 60000000 | bytes 5000000 | tf_op jit(solution)/shard_map/wave_step/pallas_call | solution.py:554
  118.1 1.4 %copy.7 = f32[1,32,36,512]{3,1,2,0:T(8,128)} copy(f32[1,32,36,512]{3,1,2,0:T(8,128)S(1)} %bitcast.2) | data formatting | bytes 4718592

commit v6 on v5

--- a/solution.py
+++ b/solution.py
@@ -102,10 +102,10 @@
             x_hbm.at[0, :, :, pl.ds(ORDER[i] * LANES, LANES)], xbuf.at[i], load_s.at[i]
         )
 
-    def store(i, half):
-        at = pl.ds(half * HALF, HALF)
+    def store(i, quarter):
+        at = pl.ds(quarter * (NTH // 4), NTH // 4)
         return pltpu.make_async_copy(
-            obuf.at[i, at], o_hbm.at[0, at, :, pl.ds(ORDER[i] * LANES, LANES)], store_s.at[i * 2 + half]
+            obuf.at[i, at], o_hbm.at[0, at, :, pl.ds(ORDER[i] * LANES, LANES)], store_s.at[i * 4 + quarter]
         )
 
     def travels(i, f, four, action):
@@ -451,10 +451,10 @@
             outs.append(u[r] - (facehi[at] * over - facelo[at] * under))
         return outs
 
-    def propagate(chunks, half):
+    def propagate(chunks, quarters):
         @pl.loop(0, NTH // 4)
         def _(t):
-            for quarter in (2 * half, 2 * half + 1):
+            for quarter in quarters:
                 j = t + 9 * quarter
                 x_pos, y_pos = quarter in (0, 3), quarter in (0, 1)
                 swept = [[None] * 4 for _ in chunks]
@@ -482,7 +482,8 @@
                         obuf[ORDER.index(col), j, at] = outs[rg] * sea
 
         for col in chunks:
-            store(ORDER.index(col), half).start()
+            for quarter in quarters:
+                store(ORDER.index(col), quarter).start()
 
     cells[0].wait()
     for i in range(4):
@@ -505,21 +506,22 @@
     interact(2)
     gather(1)
     interact(3)
+    gather(2)
     finish(0)
-    gather(2)
+    gather(3, 0)
     finish(1)
     edges()
-    gather(3, 0)
     gather(3, 1)
     finish(2)
     lon_to_right().wait_recv()
     lon_to_left().wait_recv()
-    propagate((0,), 0)
-    propagate((0,), 1)
+    propagate((0,), (0, 1))
+    propagate((0,), (2, 3))
     finish(3, 0)
-    propagate((1, 2, 3), 0)
+    propagate((1, 2, 3), (0, 1))
     finish(3, 1)
-    propagate((1, 2, 3), 1)
+    propagate((1, 2, 3), (2,))
+    propagate((1, 2, 3), (3,))
 
     for i in range(4):
         for dz in (1, 2, 3):
@@ -535,8 +537,8 @@
                 bak_up(i, m, half).wait_send()
             for m in back_dns(i):
                 bak_dn(i, m, half).wait_send()
-        store(i, 0).wait()
-        store(i, 1).wait()
+        for quarter in range(4):
+            store(i, quarter).wait()
     lon_to_right().wait_send()
     lon_to_left().wait_send()
 
@@ -585,7 +587,7 @@
             vmem((4, 8, LANES), f32),
             vmem((4, 8, LANES), f32),
             vmem((4, 8, LANES), f32),
-            dma((4,)), dma((8,)), dma((4,)),
+            dma((4,)), dma((16,)), dma((4,)),
             dma((16,)), dma((16,)),
             dma((32,)), dma((32,)),
             dma((40,)), dma((40,)),

time: 120 us -> 123 us (1.025); the launches traced: 120 us -> 121 us
    pallas_call x1, Pallas kernels: 118 us -> 119 us  [shards(): pl.pallas_call(kernel, out_shape=jax.ShapeDtypeStruct(columns.shape, f32)...]
where the time goes in v6:
time: 123 us; the launch traced here: 121 us
  Pallas kernels  119 us (97%)
  local copies, waits for them, and re-layouts  1.41 us (1%)
    pallas_call x1, Pallas kernels, shards(): pl.pallas_call(kernel, out_shape=jax.ShapeDtypeStruct(columns.shape, f32)...  119 us

profile of v6, /device:TPU:448, one launch (start us, length us, event | category | flops | bytes accessed | tf_op | source)
XLA Modules:
  0.0 120.8 jit_solution(6492463489250657659)
XLA Ops:
  0.0 119.4 %wave_step.1 = f32[1,36,32,512]{3,2,1,0:T(8,128)S(1)} custom-call(f32[8,128]{1,0:T(8,128)} %constant.2.clone.tab_hbm, f32[1,36,32,512]{3,2,1,0:T(8,128)} %bitcast.3, f32[32,512]{1,0:T(8,128)} %uw_hbm.1, f32[32,512]{1,0:T(8,128)} %wd_hbm.1, s32[32,512]{1,0:T(8,128)} %mk_hbm.1), custom_call_target="tpu_custom_call" | custom-call | flops 60000000 | bytes 5000000 | tf_op jit(solution)/shard_map/wave_step/pallas_call | solution.py:556
  119.4 1.4 %copy.7 = f32[1,32,36,512]{3,1,2,0:T(8,128)} copy(f32[1,32,36,512]{3,1,2,0:T(8,128)S(1)} %bitcast.2) | data formatting | bytes 4718592

commit v7 on v6

--- a/solution.py
+++ b/solution.py
@@ -501,16 +501,16 @@
     forward(2)
     interact(1)
     grow(3)
+    forward(3)
     gather(0)
-    forward(3)
     interact(2)
     gather(1)
     interact(3)
+    finish(0)
     gather(2)
-    finish(0)
-    gather(3, 0)
     finish(1)
     edges()
+    gather(3, 0)
     gather(3, 1)
     finish(2)
     lon_to_right().wait_recv()

time: 123 us -> 121 us (0.984); the launches traced: 121 us -> 121 us
  no operation moved by 1% of the time
where the time goes in v7:
time: 121 us
  Pallas kernels  119 us (98%)
  local copies, waits for them, and re-layouts  1.41 us (1%)
    pallas_call x1, Pallas kernels, shards(): pl.pallas_call(kernel, out_shape=jax.ShapeDtypeStruct(columns.shape, f32)...  119 us

profile of v7, /device:TPU:448, one launch (start us, length us, event | category | flops | bytes accessed | tf_op | source)
XLA Modules:
  0.0 120.8 jit_solution(11335141473406554281)
XLA Ops:
  0.0 119.4 %wave_step.1 = f32[1,36,32,512]{3,2,1,0:T(8,128)S(1)} custom-call(f32[8,128]{1,0:T(8,128)} %constant.2.clone.tab_hbm, f32[1,36,32,512]{3,2,1,0:T(8,128)} %bitcast.3, f32[32,512]{1,0:T(8,128)} %uw_hbm.1, f32[32,512]{1,0:T(8,128)} %wd_hbm.1, s32[32,512]{1,0:T(8,128)} %mk_hbm.1), custom_call_target="tpu_custom_call" | custom-call | flops 60000000 | bytes 5000000 | tf_op jit(solution)/shard_map/wave_step/pallas_call | solution.py:556
  119.4 1.4 %copy.7 = f32[1,32,36,512]{3,1,2,0:T(8,128)} copy(f32[1,32,36,512]{3,1,2,0:T(8,128)S(1)} %bitcast.2) | data formatting | bytes 4718592

commit v8 on v7

--- a/solution.py
+++ b/solution.py
@@ -501,8 +501,8 @@
     forward(2)
     interact(1)
     grow(3)
+    gather(0)
     forward(3)
-    gather(0)
     interact(2)
     gather(1)
     interact(3)

time: 121 us -> 121 us (level)
  no operation moved by 1% of the time
where the time goes in v8:
time: 121 us
  Pallas kernels  119 us (98%)
  local copies, waits for them, and re-layouts  1.41 us (1%)
    pallas_call x1, Pallas kernels, shards(): pl.pallas_call(kernel, out_shape=jax.ShapeDtypeStruct(columns.shape, f32)...  119 us

profile of v8, /device:TPU:448, one launch (start us, length us, event | category | flops | bytes accessed | tf_op | source)
XLA Modules:
  0.0 120.8 jit_solution(6466889775734485354)
XLA Ops:
  0.0 119.4 %wave_step.1 = f32[1,36,32,512]{3,2,1,0:T(8,128)S(1)} custom-call(f32[8,128]{1,0:T(8,128)} %constant.2.clone.tab_hbm, f32[1,36,32,512]{3,2,1,0:T(8,128)} %bitcast.3, f32[32,512]{1,0:T(8,128)} %uw_hbm.1, f32[32,512]{1,0:T(8,128)} %wd_hbm.1, s32[32,512]{1,0:T(8,128)} %mk_hbm.1), custom_call_target="tpu_custom_call" | custom-call | flops 60000000 | bytes 5000000 | tf_op jit(solution)/shard_map/wave_step/pallas_call | solution.py:556
  119.4 1.4 %copy.7 = f32[1,32,36,512]{3,1,2,0:T(8,128)} copy(f32[1,32,36,512]{3,1,2,0:T(8,128)S(1)} %bitcast.2) | data formatting | bytes 4718592
